TPU v7x, 256 devices: a whole 4x4x8 slice. The times are simulated.
256 devices in a mesh: lon: 16 (over y_hi, z), lat: 4 (over x), head: 4 (over y_lo, core).
Axes of the slice: x: 4, y: 4 (y_hi: 2, y_lo: 2; y = y_hi * 2 + y_lo), z: 8, core: 2. Of those that a mesh axis runs over, the one named last changes fastest.
Arguments:
- tokens: bfloat16 [2, 24, 384, 1024], P(None, 'lat', 'lon'), may hold values from -6 to 6
- norm_gain: float32 [1024], replicated, may hold values from 0.5 to 1.5
- w_qkv: bfloat16 [1024, 3072], P(None, 'head'), may hold values from -0.1875 to 0.1875
- w_out: bfloat16 [1024, 1024], P('head'), may hold values from -0.1875 to 0.1875
- bias_table: float32 [759, 16], P(None, 'head'), may hold values from -3 to 300
- cotangent: bfloat16 [2, 24, 384, 1024], P(None, 'lat', 'lon'), may hold values from -6 to 6
Outputs:
- layer_out: bfloat16 [2, 24, 384, 1024], P(None, 'lat', 'lon')
- grad_tokens: bfloat16 [2, 24, 384, 1024], P(None, 'lat', 'lon')
- grad_qkv: float32 [1024, 3072], P(('lon', 'lat'), 'head')
- grad_out: float32 [1024, 1024], P('head', ('lon', 'lat'))
All inputs are finite; a program needn't handle non-finite values.
Results may differ from a plain program's by a relative error of at most 0.013.
Values may be sent and summed in bfloat16 or wider, within the bound.
A program may use at most 64 MiB of HBM per device.

v0:
```python
import jax
import jax.numpy as jnp
from jax import lax
from jax.sharding import PartitionSpec as P

HEAD_DIM = 64
WLAT = 6
WLON = 12


EPSILON = 1e-05
NEG_FILL = -1e30


def extended(shard, sides, width, wrap):
    for axis, dim in sides:
        devices, length = (lax.axis_size(axis), shard.shape[dim])
        up = [(i, (i + 1) % devices) for i in range(devices if wrap else devices - 1)]
        down = [(j, i) for i, j in up]
        last = lax.slice_in_dim(shard, length - width, length, axis=dim)
        first = lax.slice_in_dim(shard, 0, width, axis=dim)
        before = lax.ppermute(last, axis, up)
        after = lax.ppermute(first, axis, down)
        shard = jnp.concatenate([before, shard, after], axis=dim)
    return shard


def normalize(values, norm_gain):
    floats = values.astype(jnp.float32)
    center = floats - jnp.mean(floats, axis=-1, keepdims=True)
    inverse = lax.rsqrt(jnp.mean(center * center, axis=-1, keepdims=True) + EPSILON)
    scaled = center * inverse
    return ((scaled * norm_gain).astype(jnp.bfloat16), scaled, inverse)


def step_onehot(count):
    position = jnp.arange(count, dtype=jnp.int32)
    offset = position[:, None] - position[None, :] + count - 1
    return (offset[:, :, None] == jnp.arange(2 * count - 1, dtype=jnp.int32)[None, None, :]).astype(
        jnp.float32
    )


def window_bias(bias_table, level_count):
    local_heads = bias_table.shape[1]
    table_grid = bias_table.reshape(2 * level_count - 1, 2 * WLAT - 1, 2 * WLON - 1, local_heads)
    window_size = level_count * WLAT * WLON
    expanded = jnp.einsum(
        "yvko,ezy,nwv,fck->oenfzwc",
        table_grid,
        step_onehot(level_count),
        step_onehot(WLAT),
        step_onehot(WLON),
        precision=lax.Precision.HIGHEST,
    )
    return expanded.reshape(local_heads, window_size, window_size)


def to_windows(field):
    level_count, lat_count, lon_count, channels = field.shape
    split = field.reshape(level_count, lat_count // WLAT, WLAT, lon_count // WLON, WLON, channels)
    return split.transpose(1, 3, 0, 2, 4, 5).reshape(-1, level_count * WLAT * WLON, channels)


def from_windows(blocks, level_count, lat_count, lon_count):
    channels = blocks.shape[-1]
    split = blocks.reshape(lat_count // WLAT, lon_count // WLON, level_count, WLAT, WLON, channels)
    return split.transpose(2, 0, 3, 1, 4, 5).reshape(level_count, lat_count, lon_count, channels)


def attend(query_part, key_part, value_part, grad_part, rel_bias, allowed):
    scale = HEAD_DIM ** (-0.5)
    scores = (
        jnp.einsum("wqhe,wkhe->whqk", query_part, key_part, preferred_element_type=jnp.float32)
        * scale
        + rel_bias[None]
    )
    scores = jnp.where(allowed[:, None], scores, NEG_FILL)
    peak = jnp.max(scores, axis=-1, keepdims=True)
    raised = jnp.exp(scores - peak)
    prob_full = raised / jnp.sum(raised, axis=-1, keepdims=True)
    prob_half = prob_full.astype(jnp.bfloat16)
    attended = jnp.einsum(
        "whqk,wkhe->wqhe", prob_half, value_part, preferred_element_type=jnp.float32
    ).astype(jnp.bfloat16)
    grad_prob = jnp.einsum(
        "wqhe,wkhe->whqk", grad_part, value_part, preferred_element_type=jnp.float32
    )
    row_term = jnp.sum(prob_full * grad_prob, axis=-1, keepdims=True)
    grad_score = (prob_full * (grad_prob - row_term) * scale).astype(jnp.bfloat16)
    grad_query = jnp.einsum(
        "whqk,wkhe->wqhe", grad_score, key_part, preferred_element_type=jnp.float32
    )
    grad_key = jnp.einsum(
        "whqk,wqhe->wkhe", grad_score, query_part, preferred_element_type=jnp.float32
    )
    grad_value = jnp.einsum(
        "whqk,wqhe->wkhe", prob_half, grad_part, preferred_element_type=jnp.float32
    )
    return (attended, jnp.stack([grad_query, grad_key, grad_value], axis=3).astype(jnp.bfloat16))


def widen(packed):
    around_lon = extended(packed, (("lon", 3),), WLON // 2, True)
    return extended(around_lon, (("lat", 2),), WLAT // 2, False)


def sum_groups(term):
    return lax.psum(term.astype(jnp.bfloat16), "head").astype(jnp.float32)


def body(tokens, norm_gain, w_qkv, w_out, bias_table, cotangent):
    level_count, lat_cells, lon_cells, width = tokens.shape
    local_heads = bias_table.shape[1]
    group_width = w_out.shape[0]
    margin_lat = WLAT // 2
    margin_lon = WLON // 2
    ext_lat = lat_cells + 2 * margin_lat
    ext_lon = lon_cells + 2 * margin_lon
    own_cells = level_count * lat_cells * lon_cells
    ext_cells = level_count * ext_lat * ext_lon
    window_size = level_count * WLAT * WLON
    flat_tokens = tokens.reshape(own_cells, width)
    flat_grad = cotangent.reshape(own_cells, width)
    widened = widen(jnp.stack([tokens, cotangent]))
    ext_normed, ext_scaled, ext_inverse = normalize(widened[0], norm_gain)
    qkv_flat = jnp.dot(
        ext_normed.reshape(ext_cells, width), w_qkv, preferred_element_type=jnp.float32
    ).astype(jnp.bfloat16)
    dout_flat = jnp.einsum(
        "cd,fd->cf", widened[1].reshape(ext_cells, width), w_out, preferred_element_type=jnp.float32
    ).astype(jnp.bfloat16)
    joined = jnp.concatenate([qkv_flat, dout_flat], axis=1).reshape(
        level_count, ext_lat, ext_lon, 4 * group_width
    )
    normed = ext_normed[
        :, margin_lat : margin_lat + lat_cells, margin_lon : margin_lon + lon_cells
    ].reshape(own_cells, width)
    scaled = ext_scaled[
        :, margin_lat : margin_lat + lat_cells, margin_lon : margin_lon + lon_cells
    ].reshape(own_cells, width)
    inverse = ext_inverse[
        :, margin_lat : margin_lat + lat_cells, margin_lon : margin_lon + lon_cells
    ].reshape(own_cells, 1)
    blocks = to_windows(joined)
    window_count = blocks.shape[0]
    qkv_part = blocks[:, :, : 3 * group_width].reshape(
        window_count, window_size, local_heads, 3, HEAD_DIM
    )
    grad_part = blocks[:, :, 3 * group_width :].reshape(
        window_count, window_size, local_heads, HEAD_DIM
    )
    lat_blocks = ext_lat // WLAT
    lon_blocks = ext_lon // WLON
    lat_pos = jnp.arange(window_size, dtype=jnp.int32) // WLON % WLAT
    cell_row = (
        lax.axis_index("lat") * lat_cells
        - margin_lat
        + jnp.arange(lat_blocks, dtype=jnp.int32)[:, None] * WLAT
        + lat_pos[None, :]
    )
    inside = (cell_row >= 0) & (cell_row < lat_cells * lax.axis_size("lat"))
    allowed = inside[:, :, None] == inside[:, None, :]
    allowed = jnp.broadcast_to(
        allowed[:, None], (lat_blocks, lon_blocks, window_size, window_size)
    ).reshape(window_count, window_size, window_size)
    rel_bias = window_bias(bias_table, level_count)
    attended, dstack = attend(
        qkv_part[:, :, :, 0],
        qkv_part[:, :, :, 1],
        qkv_part[:, :, :, 2],
        grad_part,
        rel_bias,
        allowed,
    )
    merged = jnp.concatenate(
        [
            attended.reshape(window_count, window_size, group_width),
            dstack.reshape(window_count, window_size, 3 * group_width),
        ],
        axis=2,
    )
    ext_field = from_windows(merged, level_count, ext_lat, ext_lon)
    own_result = ext_field[
        :, margin_lat : margin_lat + lat_cells, margin_lon : margin_lon + lon_cells
    ].reshape(own_cells, 4 * group_width)
    own_attended = own_result[:, :group_width]
    own_dqkv = own_result[:, group_width:]
    term_qkv = jnp.einsum("cd,cf->df", normed, own_dqkv, preferred_element_type=jnp.float32)
    term_out = jnp.einsum("ce,cd->ed", own_attended, flat_grad, preferred_element_type=jnp.float32)
    grad_qkv, grad_out = (
        lax.psum_scatter(term_qkv, ("lon", "lat"), scatter_dimension=0, tiled=True),
        lax.psum_scatter(term_out, ("lon", "lat"), scatter_dimension=1, tiled=True),
    )
    out_term = jnp.dot(own_attended, w_out, preferred_element_type=jnp.float32)
    in_term = jnp.einsum("cf,df->cd", own_dqkv, w_qkv, preferred_element_type=jnp.float32)
    residual = flat_tokens.astype(jnp.float32)
    upstream = flat_grad.astype(jnp.float32)
    layer_out = (residual + sum_groups(out_term)).astype(jnp.bfloat16)
    scaled_grad = sum_groups(in_term) * norm_gain
    mean_grad = jnp.mean(scaled_grad, axis=-1, keepdims=True)
    mean_mixed = jnp.mean(scaled_grad * scaled, axis=-1, keepdims=True)
    grad_tokens = (upstream + (scaled_grad - mean_grad - scaled * mean_mixed) * inverse).astype(
        jnp.bfloat16
    )
    return (
        layer_out.reshape(level_count, lat_cells, lon_cells, width),
        grad_tokens.reshape(level_count, lat_cells, lon_cells, width),
        grad_qkv,
        grad_out,
    )


def solution(mesh):
    in_specs = (
        P(None, "lat", "lon", None),
        P(),
        P(None, "head"),
        P("head", None),
        P(None, "head"),
        P(None, "lat", "lon", None),
    )
    out_specs = (
        P(None, "lat", "lon", None),
        P(None, "lat", "lon", None),
        P(("lon", "lat"), "head"),
        P("head", ("lon", "lat")),
    )
    return jax.shard_map(body, mesh=mesh, in_specs=in_specs, out_specs=out_specs, check_vma=False)
```

profile of v0, /device:TPU:1, one launch (start us, length us, event | category | flops | bytes accessed | tf_op | source)
XLA Modules:
  0.0 1323.5 jit_solution(12270602573686328488)
XLA Ops:
  8.1 2.3 pad_maximum_fusion.5
  10.4 2.5 collective-permute-start
  12.9 6.7 collective-permute-start.1
  19.5 1.5 reshape.237
  21.0 1.6 convolution_bitcast_fusion.2
  22.6 5.2 convolution_bitcast_fusion.1
  29.8 1.9 copy.73
  31.6 1.8 copy.74
  34.8 4.9 collective-permute-start.2
  39.7 7.7 convolution_bitcast_fusion
  47.4 8.6 copy.106
  56.0 4.5 reshape.254
  61.3 1.4 copy.76
  62.7 1.4 copy.75
  65.4 1.8 copy-done.1
  67.7 2.2 multiply_reduce_fusion
  69.9 5.3 slice_convert_fusion
  75.4 4.8 reshape.247
  80.2 3.7 reshape_squeeze.3
  83.9 2.1 convolution_convert_fusion.4
  86.1 3.6 fusion.24
  89.7 1.5 pad_maximum_fusion.3
  91.2 3.8 reshape_reshape.3
  94.9 3.5 copy.77
  98.4 3.8 reshape.235
  102.2 2.5 slice.72
  105.0 3.8 copy.78
  108.9 4.9 fusion.72
  113.8 3.7 fusion.37
  117.5 1.6 fusion.38
  119.1 3.7 fusion.43
  122.8 7.6 fusion.34
  130.4 7.7 fusion.31
  138.1 1.6 copy.87
  139.7 1.4 concatenate.18
  141.1 3.6 pad_maximum_fusion.1
  144.7 6.3 copy.92
  151.1 7.1 convert_element_type.85
  158.2 1.8 maximum_bitcast_fusion
  160.0 1.9 copy.93
  162.5 1.5 convolution_convert_fusion.2
  165.2 1.5 fusion.48
  167.0 2.1 fusion.2
  169.3 2.7 fusion.45
  172.1 41.9 %all-reduce.3.cloned.1.call-done = (bf16[288,1024]{1,0:T(8,128)(2,1)}, bf16[288,1024]{1,0:T(8,128)(2,1)}) async-done(((bf16[288,1024]{1,0:T(8,128)(2,1)}, bf16[288,1024]{1,0:T(8,128)(2,1)}), (bf16[288,1024]{1,0:T(8,128)(2,1)}, bf16[288,1024]{1,0:T(8,128)(2,1)})) %all-reduce.3.cloned.1.call-update) | async-done | bytes 1179664 | tf_op jit(solution)/shard_map/psum | solution.py:109
  215.4 2.9 fusion.39
  218.2 261.4 %reduce-scatter.5.cloned.1.call-done = f32[256,16]{0,1:T(8,128)} async-done(((f32[256,1024]{0,1:T(8,128)}), f32[256,16]{0,1:T(8,128)}) %reduce-scatter.5.cloned.1.call-update) | async-done | bytes 16400 | tf_op jit(solution)/shard_map/reduce_scatter | solution.py:193
  479.6 836.5 %reduce-scatter.3.cloned.1.call-done = f32[16,768]{1,0:T(8,128)} async-done(((f32[1024,768]{1,0:T(8,128)}), f32[16,768]{1,0:T(8,128)}) %reduce-scatter.3.cloned.1.call-update) | async-done | bytes 49168 | tf_op jit(solution)/shard_map/reduce_scatter | solution.py:192
  (62 shorter events, 10.1 us)
Async XLA Ops:
  8.0 78.1 %copy-start = (bf16[1024,768]{1,0:T(8,128)(2,1)S(1)}, bf16[1024,768]{1,0:T(8,128)(2,1)}, u32[]{:S(2)}) copy-start(bf16[1024,768]{1,0:T(8,128)(2,1)} %param.8) | copy-start | bytes 4718596
  8.0 206.0 %all-reduce.3.cloned.1.call-start = ((), (), s32[]{:S(2)}) async-start(), calls=%async_computation.4 | async-start | bytes 2359296 | tf_op jit(solution)/shard_map/psum | solution.py:109
  10.4 18.1 %copy-start.2 = (bf16[2,6,24,1024]{3,2,1,0:T(8,128)(2,1)S(1)}, bf16[2,6,24,1024]{3,2,1,0:T(8,128)(2,1)}, u32[]{:S(2)}) copy-start(bf16[2,6,24,1024]{3,2,1,0:T(8,128)(2,1)} %param.11) | copy-start | bytes 1769476
  10.4 18.1 %copy-start.3 = (bf16[2,6,24,1024]{3,2,1,0:T(8,128)(2,1)S(1)}, bf16[2,6,24,1024]{3,2,1,0:T(8,128)(2,1)}, u32[]{:S(2)}) copy-start(bf16[2,6,24,1024]{3,2,1,0:T(8,128)(2,1)} %param.6) | copy-start | bytes 1769476
  10.4 18.1 %collective-permute-start = (bf16[2,2,6,6,1024]{4,3,2,1,0:T(8,128)(2,1)}, bf16[2,2,6,6,1024]{4,3,2,1,0:T(8,128)(2,1)S(1)}, u32[]{:S(2)}, u32[]{:S(2)}) collective-permute-start(bf16[2,2,6,6,1024]{4,3,2,1,0:T(8,128)(2,1)} %get-tuple-element.14), channel_id=1, source_target_pairs={{0,16},{16,32},{32,48},{48,64},{64,80},{80,96},{96,112},{112,128},... | collective-permute-start | bytes 884744 | tf_op jit(solution)/shard_map/ppermute | solution.py:22
  12.9 15.6 %collective-permute-start.1 = (bf16[2,2,6,6,1024]{4,3,2,1,0:T(8,128)(2,1)}, bf16[2,2,6,6,1024]{4,3,2,1,0:T(8,128)(2,1)S(1)}, u32[]{:S(2)}, u32[]{:S(2)}) collective-permute-start(bf16[2,2,6,6,1024]{4,3,2,1,0:T(8,128)(2,1)} %get-tuple-element.15), channel_id=1, source_target_pairs={{16,0},{32,16},{48,32},{64,48},{80,64},{96,80},{112,96},{128,112},... | collective-permute-start | bytes 884744 | tf_op jit(solution)/shard_map/ppermute | solution.py:23
  33.5 27.8 %collective-permute-start.3 = (bf16[2,2,3,36,1024]{4,1,3,2,0:T(2,128)(2,1)}, bf16[2,2,3,36,1024]{4,1,3,2,0:T(2,128)(2,1)}, u32[]{:S(2)}, u32[]{:S(2)}) collective-permute-start(bf16[2,2,3,36,1024]{4,1,3,2,0:T(2,128)(2,1)} %copy.74), channel_id=1, source_target_pairs={{4,0},{8,4},{12,8},{5,1},{9,5},{13,9},{6,2},{10,6},{14,10},{7,3},{... | collective-permute-start | bytes 2654216 | tf_op jit(solution)/shard_map/ppermute | solution.py:23
  34.8 27.9 %collective-permute-start.2 = (bf16[2,2,3,36,1024]{4,1,3,2,0:T(2,128)(2,1)}, bf16[2,2,3,36,1024]{4,1,3,2,0:T(2,128)(2,1)}, u32[]{:S(2)}, u32[]{:S(2)}) collective-permute-start(bf16[2,2,3,36,1024]{4,1,3,2,0:T(2,128)(2,1)} %copy.73), channel_id=1, source_target_pairs={{0,4},{4,8},{8,12},{1,5},{5,9},{9,13},{2,6},{6,10},{10,14},{3,7},{... | collective-permute-start | bytes 2654216 | tf_op jit(solution)/shard_map/ppermute | solution.py:22
  65.4 1.9 copy-start.1
  80.2 3.7 copy-start.7
  80.2 5.9 copy-start.10
  102.2 2.5 slice-start
  102.2 6.6 copy-start.9
  113.8 3.7 copy-start.11
  151.1 7.1 copy-start.6
  161.9 2.1 copy-start.8
  162.5 4.2 copy-start.4
  165.1 314.5 %reduce-scatter.5.cloned.1.call-start = ((), (), s32[]{:S(2)}) async-start(), calls=%async_computation.3 | async-start | bytes 1064960 | tf_op jit(solution)/shard_map/reduce_scatter | solution.py:193
  166.7 1149.5 %reduce-scatter.3.cloned.1.call-start = ((), (), s32[]{:S(2)}) async-start(), calls=%async_computation.2 | async-start | bytes 3194880 | tf_op jit(solution)/shard_map/reduce_scatter | solution.py:192
  167.0 2.3 copy-start.5
Sparse Core Ops, SparseCore 0:
  165.2 48.7 all-reduce.2
Sparse Core Ops, SparseCore 1:
  168.6 310.9 reduce-scatter.4
  486.6 829.4 reduce-scatter.2
where the time goes:
time: 1330 us; the launch traced here: 1320 us
  waiting for transfers between devices  1140 us (86%)
  local copies, waits for them, and re-layouts  68.5 us (5%)
  matrix products  56.2 us (4%)
  other arithmetic  26.9 us (2%)
  between operations  15.8 us (1%)
  starting transfers between devices  15.7 us (1%)
    reduce_scatter x1, waiting for transfers between devices, body(): lax.psum_scatter(term_qkv, ('lon', 'lat'), scatter_dimension=0, tiled=True)  836 us
    reduce_scatter x1, waiting for transfers between devices, body(): lax.psum_scatter(term_out, ('lon', 'lat'), scatter_dimension=1, tiled=True)  261 us
    psum x1, waiting for transfers between devices, sum_groups(): return lax.psum(term.astype(jnp.bfloat16), 'head').astype(jnp.float32)  41.9 us
  transfers between devices with their start and end apart: 7, of which 4 were waited for; matrix products, arithmetic and copies ran while one was open for 3% of the time, Pallas kernels for 0%

commit v1 on v0

v1 whole, which is shorter than its diff:
```python
import functools

import jax
import jax.numpy as jnp
import ml_dtypes
import numpy as np
from jax import lax
from jax.experimental import pallas as pl
from jax.experimental.pallas import tpu as pltpu
from jax.sharding import PartitionSpec as P

MESH = pl.DeviceIdType.MESH
HEAD_DIM = 64
LEV = 2
WLAT = 6
WLON = 12
LON = 24
WINDOW = LEV * WLAT * WLON
CELLS = LEV * WLAT * LON
EPSILON = 1e-05
NEG_FILL = -1e30
F32 = jnp.float32
BF16 = jnp.bfloat16

G_START = (0, 112, 224, 272)
G_ROWS = 320
U_START = (0, 64, 128, 160)
U_ROWS = 192
SEL = 384


def quarter(row, col):
    down, right = row >= 3, col >= 18
    part = (2 if right else 0) + (1 if down else 0)
    width = 6 if right else 18
    return part, (row % 3) * width + (col - 18 if right else col), 3 * width


def tables():
    own = np.zeros((G_ROWS, CELLS), np.float32)
    compact = np.zeros((CELLS, G_ROWS), np.float32)
    level = np.zeros((LEV, CELLS // LEV, CELLS), np.float32)
    spread = np.zeros((U_ROWS, CELLS // LEV), np.float32)
    natural = np.zeros((CELLS // LEV, U_ROWS), np.float32)
    t_start = (0, 54, 108, 126)
    for lv in range(LEV):
        for row in range(WLAT):
            for col in range(LON):
                part, index, size = quarter(row, col)
                held = G_START[part] + lv * size + index
                src_row = row + 3 if row < 3 else row - 3
                src_col = col + 6 if col < 18 else col - 18
                own[held, lv * 144 + src_row * LON + src_col] = 1
                place = (col // WLON) * WINDOW + lv * 72 + row * WLON + col % WLON
                compact[place, held] = 1
                level[lv, t_start[part] + index, place] = 1
                if lv == 0:
                    spread[U_START[part] + index, t_start[part] + index] = 1
                    natural[src_row * LON + src_col, U_START[part] + index] = 1
    select = np.zeros((SEL, WINDOW), np.float32)
    for i in range(WINDOW):
        select[(i // 72) * 253 + (i // WLON % WLAT) * 23 + i % WLON, i] = 1
    half = np.arange(WINDOW) // WLON % WLAT >= 3
    cross = (half[:, None] != half[None, :]).astype(np.float32)
    exact = [t.astype(ml_dtypes.bfloat16) for t in (own, compact, level, spread, natural, select, np.eye(128, dtype=np.float32))]
    return exact + [cross]


def dot(a, b, ca=1, cb=0):
    return lax.dot_general(a, b, (((ca,), (cb,)), ((), ())), preferred_element_type=F32)


def layer_norm(floats):
    center = floats - jnp.mean(floats, axis=-1, keepdims=True)
    inverse = lax.rsqrt(jnp.mean(center * center, axis=-1, keepdims=True) + EPSILON)
    return center * inverse, inverse


def kernel(
    nlon, nlat,
    tok_ref, cot_ref, gain_ref, wqkv_ref, wout_ref, table_ref,
    own_ref, compact_ref, level_ref, spread_ref, natural_ref, select_ref, eye_ref, cross_ref,
    layer_ref, dtok_ref, gqkv_ref, gout_ref,
    sent, held, tokc, cotc, normed, normed_t, cot_t, qkv, datt, rolled, bias, dqkv, att,
    wgt, from_x, sum_x, from_z, sum_z, from_y,
    term, from_core, to_side, from_side, result, spread_out, back, final,
    send_sem, recv_sem, out_sem,
):
    lon, lat, head = lax.axis_index("lon"), lax.axis_index("lat"), lax.axis_index("head")
    nz = nlon // 2
    y_hi, z = lon // nz, lon % nz
    kind, core = head // 2, head % 2
    lat_up, lat_down = (lat + 1) % nlat, (lat + nlat - 1) % nlat
    lon_up, lon_down = (lon + 1) % nlon, (lon + nlon - 1) % nlon
    sibling = {"head": kind * 2 + 1 - core}
    side = {"head": (1 - kind) * 2 + core}
    x_up = [{"lat": (lat + d) % nlat} for d in range(1, nlat)]
    x_down = [{"lat": (lat + nlat - d) % nlat} for d in range(1, nlat)]
    z_up = [{"lon": y_hi * nz + (z + d) % nz} for d in range(1, nz)]
    z_down = [{"lon": y_hi * nz + (z + nz - d) % nz} for d in range(1, nz)]
    far = {"lon": (1 - y_hi) * nz + z}

    sources = x_down + z_down + [
        far, sibling, side,
        {"lon": lon_up}, {"lon": lon_down},
        {"lat": lat_up, "lon": lon_up}, {"lat": lat_down, "lon": lon_down},
    ]
    barrier = pltpu.get_barrier_semaphore()
    for source in sources:
        pl.semaphore_signal(barrier, inc=1, device_id=source, device_id_type=MESH)

    count = [0]

    def remote(src, dst, target):
        index = count[0]
        count[0] += 1
        return pltpu.make_async_remote_copy(
            src_ref=src, dst_ref=dst, send_sem=send_sem.at[index], recv_sem=recv_sem.at[index],
            device_id=target, device_id_type=MESH,
        )

    started = []

    def start(copies):
        for copy in copies:
            copy.start()
        started.extend(copies)
        return copies

    for i, ref in enumerate((tok_ref, cot_ref)):
        arranged = dot(own_ref[...], ref[...]).astype(BF16)
        held[i, 0:112] = arranged[0:112]
        sent[i] = arranged[112:]
    pl.semaphore_wait(barrier, len(sources))
    parts = [(112, 112, {"lat": lat_down}), (224, 48, {"lon": lon_down}), (272, 48, {"lat": lat_down, "lon": lon_down})]
    shifted = start([
        remote(sent.at[core, pl.ds(at - 112, size)], held.at[core, pl.ds(at, size)], target) for at, size, target in parts
    ])

    for h in range(4):
        stepped = jnp.broadcast_to(table_ref[h : h + 1, :], (16, table_ref.shape[1]))
        stepped = pltpu.roll(stepped, 0, 1, stride=1, stride_axis=0)
        for step in range(LEV * WLAT):
            offset = (step // WLAT) * 253 + (step % WLAT) * 23
            shift = (offset - 379) % table_ref.shape[1]
            moved = pltpu.roll(stepped, shift, 1)
            rolled[WLON * step : WLON * step + WLON, :] = moved[0:WLON, 0:SEL]
        rest = rolled[...]
        total = jnp.zeros((WINDOW, WINDOW), F32)
        for _ in range(3):
            piece = rest.astype(BF16)
            rest = rest - piece.astype(F32)
            total = total + dot(piece, select_ref[...])
        excluded = (cross_ref[...] > 0.5) & (lat == nlat - 1)
        bias[h] = jnp.where(excluded, NEG_FILL, total)

    forwards = []
    for copy, (at, size, _) in zip(shifted, parts):
        copy.wait_recv()
        forwards += start([remote(held.at[core, pl.ds(at, size)], held.at[core, pl.ds(at, size)], sibling)])
    for copy in forwards:
        copy.wait_recv()

    tokc[...] = dot(compact_ref[...], held[0]).astype(BF16)
    cotc[...] = dot(compact_ref[...], held[1]).astype(BF16)
    for at in range(0, CELLS, 48):
        scaled, _ = layer_norm(tokc[at : at + 48, :].astype(F32))
        normed[at : at + 48, :] = (scaled * gain_ref[...]).astype(BF16)
    qkv[...] = dot(normed[...], wqkv_ref[...]).astype(BF16)
    datt[...] = dot(cotc[...], wout_ref[...], 1, 1).astype(BF16)
    for at in range(0, normed.shape[1], 128):
        normed_t[at : at + 128, :] = dot(eye_ref[...], normed[:, at : at + 128], 1, 1).astype(BF16)
        cot_t[at : at + 128, :] = dot(eye_ref[...], cotc[:, at : at + 128], 1, 1).astype(BF16)

    def attend(w, h):
        rows = pl.ds(w * WINDOW, WINDOW)
        first = 3 * HEAD_DIM * h
        query = qkv[rows, first : first + 64]
        key = qkv[rows, first + 64 : first + 128]
        value = qkv[rows, first + 128 : first + 192]
        grad = datt[rows, 64 * h : 64 * h + 64]
        scores = dot(key, query, 1, 1) * (HEAD_DIM ** -0.5) + bias[h]
        raised = jnp.exp(scores - jnp.max(scores, axis=0, keepdims=True))
        prob = raised * (1.0 / jnp.sum(raised, axis=0, keepdims=True))
        half = prob.astype(BF16)
        grad_prob = dot(value, grad, 1, 1)
        row_term = jnp.sum(prob * grad_prob, axis=0, keepdims=True)
        grad_score = (prob * (grad_prob - row_term) * (HEAD_DIM ** -0.5)).astype(BF16)
        att[rows, 64 * h : 64 * h + 64] = dot(half, value, 0, 0).astype(BF16)
        dqkv[rows, first : first + 64] = dot(grad_score, key, 0, 0).astype(BF16)
        dqkv[rows, first + 64 : first + 128] = dot(grad_score, query, 1, 0).astype(BF16)
        dqkv[rows, first + 128 : first + 192] = dot(half, grad, 1, 0).astype(BF16)

    rows_out = wgt.shape[3]
    on_x, on_z, on_y = [], [], []
    for pair in range(2):
        for h in (2 * pair, 2 * pair + 1):
            for w in range(2):
                attend(w, h)
        wide = dot(normed_t[...], dqkv[:, 384 * pair : 384 * pair + 384]).astype(BF16)
        wgt[pair, :, :, :, 0:384] = wide.reshape(nlon, nlat, rows_out, 384)
        narrow = dot(cot_t[...], att[:, 128 * pair : 128 * pair + 128]).astype(BF16)
        wgt[pair, :, :, :, 384:512] = narrow.reshape(nlon, nlat, rows_out, 128)
        on_x.append(start([
            remote(wgt.at[pair, :, target["lat"]], from_x.at[pair, d], target) for d, target in enumerate(x_up)
        ]))

    for lv in (1 - core, core):
        order = level_ref[lv]
        att_l = dot(order, att[...]).astype(BF16)
        dqkv_l = dot(order, dqkv[...]).astype(BF16)
        term[lv, 0] = dot(att_l, wout_ref[...]).astype(BF16)
        term[lv, 1] = dot(dqkv_l, wqkv_ref[...], 1, 1).astype(BF16)
        if lv is not core:
            on_core = start([remote(term.at[1 - core], from_core, sibling)])[0]
    tok_l = dot(level_ref[core], tokc[...])
    cot_l = dot(level_ref[core], cotc[...])

    def pass_x(pair):
        for copy in on_x[pair]:
            copy.wait_recv()
        total = wgt[pair, :, lat].astype(F32)
        for d in range(nlat - 1):
            total = total + from_x[pair, d].astype(F32)
        sum_x[pair] = total.astype(BF16).reshape(sum_x.shape[1:])
        on_z.append(start([
            remote(sum_x.at[pair, :, target["lon"] - y_hi * nz], from_z.at[pair, d], target) for d, target in enumerate(z_up)
        ]))

    def pass_z(pair):
        for copy in on_z[pair]:
            copy.wait_recv()
        total = sum_x[pair, :, z].astype(F32)
        for d in range(nz - 1):
            total = total + from_z[pair, d].astype(F32)
        sum_z[pair] = total.astype(BF16)
        on_y.append(start([remote(sum_z.at[pair, 1 - y_hi], from_y.at[pair], far)])[0])

    def pass_y(pair):
        on_y[pair].wait_recv()
        total = sum_z[pair, y_hi].astype(F32) + from_y[pair].astype(F32)
        gqkv_ref[:, 384 * pair : 384 * pair + 384] = total[:, 0:384]
        gout_ref[:, 128 * pair : 128 * pair + 128] = total[:, 384:512]

    on_core.wait_recv()
    to_side[...] = (term[core, 1 - kind].astype(F32) + from_core[1 - kind].astype(F32)).astype(BF16)
    on_side = start([remote(to_side, from_side, side)])[0]
    pass_x(0)
    on_side.wait_recv()
    total = term[core, kind].astype(F32) + from_core[kind].astype(F32) + from_side[...].astype(F32)

    @pl.when(kind == 0)
    def _():
        result[...] = (tok_l + total).astype(BF16)

    @pl.when(kind == 1)
    def _():
        scaled, inverse = layer_norm(tok_l)
        grad = total * gain_ref[...]
        mean_grad = jnp.mean(grad, axis=-1, keepdims=True)
        mean_mixed = jnp.mean(grad * scaled, axis=-1, keepdims=True)
        result[...] = (cot_l + (grad - mean_grad - scaled * mean_mixed) * inverse).astype(BF16)

    spread_out[...] = dot(spread_ref[...], result[...]).astype(BF16)
    back[0:64] = spread_out[0:64]
    returned = start([
        remote(spread_out.at[pl.ds(at, size)], back.at[pl.ds(at, size)], target)
        for at, size, target in ((64, 64, {"lat": lat_up}), (128, 32, {"lon": lon_up}), (160, 32, {"lat": lat_up, "lon": lon_up}))
    ])
    pass_x(1)
    pass_z(0)
    for copy in returned:
        copy.wait_recv()
    final[kind, core] = dot(natural_ref[...], back[...]).astype(BF16)
    own_side, own_core = start([
        remote(final.at[kind, core], final.at[kind, core], side),
        remote(final.at[kind, core], final.at[kind, core], sibling),
    ])
    pass_z(1)
    pass_y(0)
    own_side.wait_recv()
    other_core = start([remote(final.at[1 - kind, core], final.at[1 - kind, core], sibling)])[0]
    pass_y(1)
    own_core.wait_recv()
    other_core.wait_recv()
    outs = [
        pltpu.make_async_copy(final.at[0], layer_ref, out_sem.at[0]),
        pltpu.make_async_copy(final.at[1], dtok_ref, out_sem.at[1]),
    ]
    for copy in outs:
        copy.start()
    for copy in started:
        copy.wait_send()
    for copy in outs:
        copy.wait()


def body(tokens, norm_gain, w_qkv, w_out, bias_table, cotangent):
    nlon, nlat = lax.axis_size("lon"), lax.axis_size("lat")
    nz = nlon // 2
    width = tokens.shape[-1]
    rows = width // (nlon * nlat)
    table = jnp.pad(bias_table.T, ((0, 4), (0, 768 - bias_table.shape[0])))
    vmem = pl.BlockSpec(memory_space=pltpu.VMEM)
    hbm = pl.BlockSpec(memory_space=pl.ANY)
    copies = 3 + 3 + 2 * (nlat - 1) + 2 * (nz - 1) + 2 + 2 + 3 + 3
    shape = lambda *dims: pltpu.VMEM(dims, BF16)
    layer, dtok, gqkv, gout = pl.pallas_call(
        functools.partial(kernel, nlon, nlat),
        out_shape=(
            jax.ShapeDtypeStruct((LEV, CELLS // LEV, width), BF16),
            jax.ShapeDtypeStruct((LEV, CELLS // LEV, width), BF16),
            jax.ShapeDtypeStruct((rows, 768), F32),
            jax.ShapeDtypeStruct((rows, 256), F32),
        ),
        in_specs=[vmem] * 14,
        out_specs=(hbm, hbm, vmem, vmem),
        scratch_shapes=[
            shape(2, G_ROWS - 112, width),
            shape(2, G_ROWS, width),
            shape(CELLS, width),
            shape(CELLS, width),
            shape(CELLS, width),
            shape(width, CELLS),
            shape(width, CELLS),
            shape(CELLS, 768),
            shape(CELLS, 256),
            pltpu.VMEM((WINDOW, SEL), F32),
            pltpu.VMEM((4, WINDOW, WINDOW), F32),
            shape(CELLS, 768),
            shape(CELLS, 256),
            shape(2, nlon, nlat, rows, 512),
            shape(2, nlat - 1, nlon, rows, 512),
            shape(2, 2, nz, rows, 512),
            shape(2, max(nz - 1, 1), 2, rows, 512),
            shape(2, 2, rows, 512),
            shape(2, rows, 512),
            shape(LEV, 2, CELLS // LEV, width),
            shape(2, CELLS // LEV, width),
            shape(CELLS // LEV, width),
            shape(CELLS // LEV, width),
            shape(CELLS // LEV, width),
            shape(U_ROWS, width),
            shape(U_ROWS, width),
            shape(2, LEV, CELLS // LEV, width),
            pltpu.SemaphoreType.DMA((copies,)),
            pltpu.SemaphoreType.DMA((copies,)),
            pltpu.SemaphoreType.DMA((2,)),
        ],
        compiler_params=pltpu.CompilerParams(
            collective_id=0, has_side_effects=True, vmem_limit_bytes=56 * 1024 * 1024
        ),
    )(
        tokens.reshape(CELLS, width), cotangent.reshape(CELLS, width), norm_gain.reshape(1, width),
        w_qkv, w_out, table, *[jnp.asarray(t) for t in tables()],
    )
    field = (LEV, WLAT, LON, width)
    return layer.reshape(field), dtok.reshape(field), gqkv, gout.T


def solution(mesh):
    in_specs = (
        P(None, "lat", "lon", None),
        P(),
        P(None, "head"),
        P("head", None),
        P(None, "head"),
        P(None, "lat", "lon", None),
    )
    out_specs = (
        P(None, "lat", "lon", None),
        P(None, "lat", "lon", None),
        P(("lon", "lat"), "head"),
        P("head", ("lon", "lat")),
    )
    return jax.shard_map(body, mesh=mesh, in_specs=in_specs, out_specs=out_specs, check_vma=False)
```

time: 1330 us -> 75.7 us (0.06)
  waiting for transfers between devices: 1140 us -> 0 us
  Pallas kernels: 0 us -> 69.5 us
  local copies, waits for them, and re-layouts: 68.5 us -> 5.35 us
  matrix products: 56.2 us -> 0 us
  other arithmetic: 26.9 us -> 0 us
  starting transfers between devices: 15.7 us -> 0 us
  between operations: 15.8 us -> 0.67 us
    reduce_scatter x2 -> x0, waiting for transfers between devices: 1100 us -> none  [the longest x1 836 us: body(): lax.psum_scatter(term_qkv, ('lon', 'lat'), scatter_dimension=0, tiled=True)]
    pallas_call x0 -> x1, Pallas kernels: none -> 69.5 us  [body(): pl.pallas_call(functools.partial(kernel, nlon, nlat), out_shape=(jax.Shap...]
    dot_general x14 -> x0, matrix products: 51.3 us -> none  [the longest x3 14.5 us: window_bias(): jnp.einsum('yvko,ezy,nwv,fck->oenfzwc', table_grid, step_onehot(level_cou...]
    psum x1 -> x0, waiting for transfers between devices: 41.9 us -> none  [sum_groups(): return lax.psum(term.astype(jnp.bfloat16), 'head').astype(jnp.float32)]
    ppermute x4 -> x0, starting transfers between devices: 15.3 us -> none  [the longest x2 7.93 us: extended(): after = lax.ppermute(first, axis, down)]
    another operation x3 -> x0, local copies, waits for them, and re-layouts: 13.9 us -> none  [the longest x1 6.32 us: attend(): jnp.stack([grad_query, grad_key, grad_value], axis=3).astype(jnp.bfloat16)]
    convert_element_type x3 -> x0, local copies, waits for them, and re-layouts: 13.5 us -> none  [the longest x1 7.12 us: attend(): jnp.stack([grad_query, grad_key, grad_value], axis=3).astype(jnp.bfloat16)]
  transfers between devices with their start and end apart: 7 -> 0, of which waited for: 4 -> 0; matrix products, arithmetic and copies ran while one was open for 3% -> 0% of each run, Pallas kernels for 0% -> 0%
where the time goes in v1:
time: 75.7 us; the launch traced here: 75.6 us
  Pallas kernels  69.5 us (92%)
  local copies, waits for them, and re-layouts  5.35 us (7%)
    pallas_call x1, Pallas kernels, body(): pl.pallas_call(functools.partial(kernel, nlon, nlat), out_shape=(jax.Shap...  69.5 us
    unnamed x10, local copies, waits for them, and re-layouts  4.03 us

profile of v1, /device:TPU:1, one launch (start us, length us, event | category | flops | bytes accessed | tf_op | source)
XLA Modules:
  0.0 75.6 jit_solution(10253514993862474161)
XLA Ops:
  0.6 1.3 %pad.4.table_ref = f32[8,768]{1,0:T(8,128)} pad(f32[4,759]{1,0:T(4,128)} %bitcast.12, f32[]{:T(128)} %constant.18.clone.1), padding=0_4x0_9 | pad | bytes 36724 | tf_op jit(solution)/shard_map/jit(_pad)/pad | solution.py:303
  2.0 69.5 %shard_map.165 = (bf16[2,144,1024]{2,1,0:T(8,128)(2,1)}, bf16[2,144,1024]{2,1,0:T(8,128)(2,1)}, f32[16,768]{1,0:T(8,128)}, f32[16,256]{1,0:T(8,128)}) custom-call(bf16[288,1024]{1,0:T(8,128)(2,1)} %bitcast.9, bf16[288,1024]{1,0:T(8,128)(2,1)} %bitcast.10, f32[1,1024]{1,0:T(1,128)} %bitcast.13, bf16[1024,768]{1,0:T(8,128)(2,1)} %wqkv_ref.1, ...), custom_call_target="tpu_custom_call" | custom-call | tf_op jit(solution)/shard_map/pallas_call | solution.py:308
  71.5 0.0 copy-start
  71.5 0.0 copy-start.1
  71.5 0.0 copy-start.2
  71.5 2.0 %copy.22 = bf16[2,6,24,1024]{3,2,1,0:T(8,128)(2,1)} copy(bf16[2,6,24,1024]{3,2,1,0:T(8,128)(2,1)} %bitcast.8) | data formatting | bytes 1179648
  73.5 0.0 copy-done
  73.5 0.8 %copy.23 = bf16[2,6,24,1024]{3,2,1,0:T(8,128)(2,1)} copy(bf16[2,6,24,1024]{3,2,1,0:T(8,128)(2,1)S(1)} %bitcast.7) | data formatting | bytes 1179648
  74.3 0.0 copy-done.1
  74.3 0.6 copy.24
  74.9 0.0 copy-done.2
  74.9 0.6 copy.25
Async XLA Ops:
  71.5 2.0 %copy-start = (bf16[2,144,1024]{2,1,0:T(8,128)(2,1)S(1)}, bf16[2,144,1024]{2,1,0:T(8,128)(2,1)}, u32[]{:S(2)}) copy-start(bf16[2,144,1024]{2,1,0:T(8,128)(2,1)} %get-tuple-element.9) | copy-start | bytes 1769476
  71.5 2.8 %copy-start.1 = (f32[16,768]{1,0:T(8,128)S(1)}, f32[16,768]{1,0:T(8,128)}, u32[]{:S(2)}) copy-start(f32[16,768]{1,0:T(8,128)} %get-tuple-element.18) | copy-start | bytes 147460
  71.5 3.4 %copy-start.2 = (f32[16,256]{1,0:T(8,128)S(1)}, f32[16,256]{1,0:T(8,128)}, u32[]{:S(2)}) copy-start(f32[16,256]{1,0:T(8,128)} %get-tuple-element.11) | copy-start | bytes 49156

commit v2 on v1

v2 whole, which is shorter than its diff:
```python
import functools

import jax
import jax.numpy as jnp
import ml_dtypes
import numpy as np
from jax import lax
from jax.experimental import pallas as pl
from jax.experimental.pallas import tpu as pltpu
from jax.sharding import PartitionSpec as P

MESH = pl.DeviceIdType.MESH
HEAD_DIM = 64
LEV = 2
WLAT = 6
WLON = 12
LON = 24
WINDOW = LEV * WLAT * WLON
CELLS = LEV * WLAT * LON
EPSILON = 1e-05
NEG_FILL = -1e30
F32 = jnp.float32
BF16 = jnp.bfloat16

G_START = (0, 112, 224, 272)
G_ROWS = 320
T_START = (96, 0, 54, 72)
T_AWAY = 96
T_ROWS = 160
U_START = (None, 0, 64, 96)
U_ROWS = 128
SEL = 384


def quarter(row, col):
    down, right = row >= 3, col >= 18
    part = (2 if right else 0) + (1 if down else 0)
    width = 6 if right else 18
    return part, (row % 3) * width + (col - 18 if right else col), 3 * width


def tables():
    own = np.zeros((G_ROWS, CELLS), np.float32)
    compact = np.zeros((CELLS, G_ROWS), np.float32)
    level = np.zeros((LEV, T_ROWS, CELLS), np.float32)
    spread = np.zeros((U_ROWS, T_AWAY), np.float32)
    natural = np.zeros((CELLS // LEV, T_ROWS), np.float32)
    for lv in range(LEV):
        for row in range(WLAT):
            for col in range(LON):
                part, index, size = quarter(row, col)
                held = G_START[part] + lv * size + index
                src_row = row + 3 if row < 3 else row - 3
                src_col = col + 6 if col < 18 else col - 18
                own[held, lv * 144 + src_row * LON + src_col] = 1
                place = (col // WLON) * WINDOW + lv * 72 + row * WLON + col % WLON
                compact[place, held] = 1
                level[lv, T_START[part] + index, place] = 1
                if lv == 0:
                    natural[src_row * LON + src_col, T_START[part] + index] = 1
                    if part:
                        spread[U_START[part] + index, T_START[part] + index] = 1
    select = np.zeros((SEL, WINDOW), np.float32)
    for i in range(WINDOW):
        select[(i // 72) * 253 + (i // WLON % WLAT) * 23 + i % WLON, i] = 1
    half = np.arange(WINDOW) // WLON % WLAT >= 3
    cross = (half[:, None] != half[None, :]).astype(np.float32)
    exact = [t.astype(ml_dtypes.bfloat16) for t in (own, compact, level, spread, spread.T, natural, select, np.eye(128, dtype=np.float32))]
    return exact + [cross]


def dot(a, b, ca=1, cb=0):
    return lax.dot_general(a, b, (((ca,), (cb,)), ((), ())), preferred_element_type=F32)


def layer_norm(floats):
    center = floats - jnp.mean(floats, axis=-1, keepdims=True)
    inverse = lax.rsqrt(jnp.mean(center * center, axis=-1, keepdims=True) + EPSILON)
    return center * inverse, inverse


def kernel(
    nlon, nlat,
    tok_ref, cot_ref, gain_ref, wqkv_ref, wout_ref, table_ref,
    own_ref, compact_ref, level_ref, spread_ref, gather_ref, natural_ref, select_ref, eye_ref, cross_ref,
    layer_ref, dtok_ref, gqkv_ref, gout_ref,
    sent, held, tokc, cotc, normed, normed_t, cot_t, qkv, datt, wide_table, rolled, bias, dqkv, att,
    wgt, near_x, sum_x, near_z, first_z, sum_z, last_x, sum_y, from_y,
    term, from_core, to_side, from_side, result, spread_out, back, final, fields,
    send_sem, recv_sem, out_sem,
):
    lon, lat, head = lax.axis_index("lon"), lax.axis_index("lat"), lax.axis_index("head")
    nz = nlon // 2
    y_hi, z = lon // nz, lon % nz
    kind, core = head // 2, head % 2
    lat_up, lat_down = (lat + 1) % nlat, (lat + nlat - 1) % nlat
    lon_up, lon_down = (lon + 1) % nlon, (lon + nlon - 1) % nlon
    sibling = {"head": kind * 2 + 1 - core}
    side = {"head": (1 - kind) * 2 + core}
    x_up = [{"lat": (lat + d) % nlat} for d in range(1, nlat)]
    x_down = [{"lat": (lat + nlat - d) % nlat} for d in range(1, nlat)]
    z_up = [{"lon": y_hi * nz + (z + d) % nz} for d in range(1, nz)]
    z_down = [{"lon": y_hi * nz + (z + nz - d) % nz} for d in range(1, nz)]
    far = {"lon": (1 - y_hi) * nz + z}

    sources = x_down + z_down + [
        far, sibling, side,
        {"lon": lon_up}, {"lon": lon_down},
        {"lat": lat_up, "lon": lon_up}, {"lat": lat_down, "lon": lon_down},
    ]
    barrier = pltpu.get_barrier_semaphore()
    for source in sources:
        pl.semaphore_signal(barrier, inc=1, device_id=source, device_id_type=MESH)

    count = [0]

    def remote(src, dst, target):
        index = count[0]
        count[0] += 1
        return pltpu.make_async_remote_copy(
            src_ref=src, dst_ref=dst, send_sem=send_sem.at[index], recv_sem=recv_sem.at[index],
            device_id=target, device_id_type=MESH,
        )

    started = []

    def start(copies):
        for copy in copies:
            copy.start()
        started.extend(copies)
        return copies

    for i, ref in enumerate((tok_ref, cot_ref)):
        arranged = dot(own_ref[...], ref[...]).astype(BF16)
        held[i, 0:112] = arranged[0:112]
        sent[i] = arranged[112:]
    pl.semaphore_wait(barrier, len(sources))
    diagonal = {"lat": lat_down, "lon": lon_down}
    parts = [(112, 64, {"lat": lat_down}), (224, 48, {"lon": lon_down}), (272, 48, diagonal), (176, 48, {"lat": lat_down})]
    shifted = start([
        remote(sent.at[core, pl.ds(at - 112, size)], held.at[core, pl.ds(at, size)], target) for at, size, target in parts
    ])

    wide_table[...] = jnp.zeros(wide_table.shape, F32)
    wide_table[0 : table_ref.shape[0], 0:4] = table_ref[...]
    turned = wide_table[...].T
    for h in range(4):
        stepped = jnp.broadcast_to(turned[h : h + 1, :], (16, turned.shape[1]))
        stepped = pltpu.roll(stepped, 0, 1, stride=1, stride_axis=0)
        for step in range(LEV * WLAT):
            offset = (step // WLAT) * 253 + (step % WLAT) * 23
            shift = (offset - 379) % turned.shape[1]
            moved = pltpu.roll(stepped, shift, 1)
            rolled[WLON * step : WLON * step + WLON, :] = moved[0:WLON, 0:SEL]
        rest = rolled[...]
        total = jnp.zeros((WINDOW, WINDOW), F32)
        for _ in range(3):
            piece = rest.astype(BF16)
            rest = rest - piece.astype(F32)
            total = total + dot(piece, select_ref[...])
        excluded = (cross_ref[...] > 0.5) & (lat == nlat - 1)
        bias[h] = jnp.where(excluded, NEG_FILL, total)

    forwards = []
    for copy, (at, size, _) in zip(shifted, parts):
        copy.wait_recv()
        forwards += start([remote(held.at[core, pl.ds(at, size)], held.at[core, pl.ds(at, size)], sibling)])
    for copy in forwards:
        copy.wait_recv()

    tokc[...] = dot(compact_ref[...], held[0]).astype(BF16)
    cotc[...] = dot(compact_ref[...], held[1]).astype(BF16)
    for at in range(0, CELLS, 48):
        scaled, _ = layer_norm(tokc[at : at + 48, :].astype(F32))
        normed[at : at + 48, :] = (scaled * gain_ref[...]).astype(BF16)
    qkv[...] = dot(normed[...], wqkv_ref[...]).astype(BF16)
    datt[...] = dot(cotc[...], wout_ref[...], 1, 1).astype(BF16)
    for at in range(0, normed.shape[1], 128):
        normed_t[at : at + 128, :] = dot(eye_ref[...], normed[:, at : at + 128], 1, 1).astype(BF16)
        cot_t[at : at + 128, :] = dot(eye_ref[...], cotc[:, at : at + 128], 1, 1).astype(BF16)

    def attend(w, h):
        rows = pl.ds(w * WINDOW, WINDOW)
        first = 3 * HEAD_DIM * h
        query = qkv[rows, first : first + 64]
        key = qkv[rows, first + 64 : first + 128]
        value = qkv[rows, first + 128 : first + 192]
        grad = datt[rows, 64 * h : 64 * h + 64]
        scores = dot(key, query, 1, 1) * (HEAD_DIM ** -0.5) + bias[h]
        raised = jnp.exp(scores - jnp.max(scores, axis=0, keepdims=True))
        prob = raised * (1.0 / jnp.sum(raised, axis=0, keepdims=True))
        half = prob.astype(BF16)
        grad_prob = dot(value, grad, 1, 1)
        row_term = jnp.sum(prob * grad_prob, axis=0, keepdims=True)
        grad_score = (prob * (grad_prob - row_term) * (HEAD_DIM ** -0.5)).astype(BF16)
        att[rows, 64 * h : 64 * h + 64] = dot(half, value, 0, 0).astype(BF16)
        dqkv[rows, first : first + 64] = dot(grad_score, key, 0, 0).astype(BF16)
        dqkv[rows, first + 64 : first + 128] = dot(grad_score, query, 1, 0).astype(BF16)
        dqkv[rows, first + 128 : first + 192] = dot(half, grad, 1, 0).astype(BF16)

    rows_out = wgt.shape[4]
    on_first, on_second, on_y = {}, {}, {}

    def weight(h):
        wide = dot(normed_t[...], dqkv[:, 192 * h : 192 * h + 192]).astype(BF16)
        wgt[h, :, :, :, :, 0:192] = wide.reshape(2, nz, nlat, rows_out, 192)
        narrow = dot(cot_t[...], att[:, 64 * h : 64 * h + 64]).astype(BF16)
        wgt[h, :, :, :, :, 192:256] = narrow.reshape(2, nz, nlat, rows_out, 64)
        if h == 0:
            on_first[h] = start([
                remote(wgt.at[h, :, target["lon"] - y_hi * nz], near_z.at[d], target) for d, target in enumerate(z_up)
            ])
        else:
            on_first[h] = start([
                remote(wgt.at[h, :, :, target["lat"]], near_x.at[h - 1, d], target) for d, target in enumerate(x_up)
            ])

    def second(h):
        for copy in on_first[h]:
            copy.wait_recv()
        if h == 0:
            total = wgt[h, :, z].astype(F32)
            for d in range(nz - 1):
                total = total + near_z[d].astype(F32)
            first_z[...] = total.astype(BF16)
            on_second[h] = start([
                remote(first_z.at[:, target["lat"]], last_x.at[d], target) for d, target in enumerate(x_up)
            ])
        else:
            total = wgt[h, :, :, lat].astype(F32)
            for d in range(nlat - 1):
                total = total + near_x[h - 1, d].astype(F32)
            sum_x[h - 1] = total.astype(BF16)
            on_second[h] = start([
                remote(sum_x.at[h - 1, :, target["lon"] - y_hi * nz], sum_z.at[h - 1, d], target) for d, target in enumerate(z_up)
            ])

    def third(h):
        for copy in on_second[h]:
            copy.wait_recv()
        if h == 0:
            total = first_z[:, lat].astype(F32)
            for d in range(nlat - 1):
                total = total + last_x[d].astype(F32)
        else:
            total = sum_x[h - 1, :, z].astype(F32)
            for d in range(nz - 1):
                total = total + sum_z[h - 1, d].astype(F32)
        sum_y[h] = total.astype(BF16)
        on_y[h] = start([remote(sum_y.at[h, 1 - y_hi], from_y.at[h], far)])[0]

    def last(h):
        on_y[h].wait_recv()
        total = sum_y[h, y_hi].astype(F32) + from_y[h].astype(F32)
        gqkv_ref[:, 192 * h : 192 * h + 192] = total[:, 0:192]
        gout_ref[:, 64 * h : 64 * h + 64] = total[:, 192:256]

    for h in range(4):
        for w in range(2):
            attend(w, h)
        if h < 3:
            weight(h)

    chunks = ((0, T_AWAY), (T_AWAY, T_ROWS - T_AWAY))
    on_core = []
    for lv in (1 - core, core):
        for at, size in chunks:
            order = level_ref[lv, at : at + size]
            att_l = dot(order, att[...]).astype(BF16)
            dqkv_l = dot(order, dqkv[...]).astype(BF16)
            term[lv, 0, at : at + size] = dot(att_l, wout_ref[...]).astype(BF16)
            term[lv, 1, at : at + size] = dot(dqkv_l, wqkv_ref[...], 1, 1).astype(BF16)
            if lv is not core:
                on_core += start([
                    remote(term.at[1 - core, :, pl.ds(at, size)], from_core.at[:, pl.ds(at, size)], sibling)
                ])
    on_side = []
    for copy, (at, size) in zip(on_core, chunks):
        copy.wait_recv()
        rows = pl.ds(at, size)
        to_side[rows] = (term[core, 1 - kind, rows].astype(F32) + from_core[1 - kind, rows].astype(F32)).astype(BF16)
        on_side += start([remote(to_side.at[rows], from_side.at[rows], side)])
    weight(3)

    def finish(chunk):
        at, size = chunks[chunk]
        rows = pl.ds(at, size)
        tok_l = dot(level_ref[core, at : at + size], tokc[...])
        cot_l = dot(level_ref[core, at : at + size], cotc[...])
        on_side[chunk].wait_recv()
        total = term[core, kind, rows].astype(F32) + from_core[kind, rows].astype(F32) + from_side[rows].astype(F32)

        @pl.when(kind == 0)
        def _():
            result[rows] = (tok_l + total).astype(BF16)

        @pl.when(kind == 1)
        def _():
            scaled, inverse = layer_norm(tok_l)
            grad = total * gain_ref[...]
            mean_grad = jnp.mean(grad, axis=-1, keepdims=True)
            mean_mixed = jnp.mean(grad * scaled, axis=-1, keepdims=True)
            result[rows] = (cot_l + (grad - mean_grad - scaled * mean_mixed) * inverse).astype(BF16)

    def share(chunk):
        rows = pl.ds(*chunks[chunk])
        return start([
            remote(final.at[kind, core, rows], final.at[kind, core, rows], side),
            remote(final.at[kind, core, rows], final.at[kind, core, rows], sibling),
        ])

    def relay(chunk, copy):
        rows = pl.ds(*chunks[chunk])
        copy.wait_recv()
        return start([remote(final.at[1 - kind, core, rows], final.at[1 - kind, core, rows], sibling)])[0]

    outs = []

    def place(k, lv):
        fields[k, lv] = dot(natural_ref[...], final[k, lv]).astype(BF16)
        for index, ref in enumerate((layer_ref, dtok_ref)):
            @pl.when(k == index)
            def _():
                pltpu.make_async_copy(fields.at[k, lv], ref.at[lv], out_sem.at[len(outs)]).start()
        outs.append(pltpu.make_async_copy(fields.at[k, lv], layer_ref.at[lv], out_sem.at[len(outs)]))

    finish(0)
    spread_out[...] = dot(spread_ref[...], result[0:T_AWAY]).astype(BF16)
    returned = start([
        remote(spread_out.at[pl.ds(at, size)], back.at[pl.ds(at, size)], target)
        for at, size, target in ((0, 64, {"lat": lat_up}), (64, 32, {"lon": lon_up}), (96, 32, {"lat": lat_up, "lon": lon_up}))
    ])
    finish(1)
    final[kind, core, T_AWAY:T_ROWS] = result[T_AWAY:T_ROWS]
    shared = [share(1)]
    second(1)
    for copy in returned:
        copy.wait_recv()
    final[kind, core, 0:T_AWAY] = dot(gather_ref[...], back[...]).astype(BF16)
    shared = [share(0)] + shared
    place(kind, core)
    second(0)
    relayed = [relay(1, shared[1][0])]
    second(2)
    third(1)
    relayed.append(relay(0, shared[0][0]))
    place(1 - kind, core)
    for _, copy in shared:
        copy.wait_recv()
    place(kind, 1 - core)
    third(0)
    for copy in relayed:
        copy.wait_recv()
    place(1 - kind, 1 - core)
    second(3)
    third(2)
    last(1)
    last(0)
    third(3)
    last(2)
    last(3)
    for copy in started:
        copy.wait_send()
    for copy in outs:
        copy.wait()


def finisher(layer_in, dtok_in, gqkv_in, gout_in, layer_out, dtok_out, gqkv_out, gout_out, turned, sem):
    copies = [
        pltpu.make_async_copy(src, dst, sem.at[i])
        for i, (src, dst) in enumerate(((layer_in, layer_out), (dtok_in, dtok_out), (gqkv_in, gqkv_out)))
    ]
    for copy in copies:
        copy.start()
    turned[0 : gout_in.shape[0], :] = gout_in[...]
    gout_out[...] = turned[...].T[:, 0 : gout_in.shape[0]]
    for copy in copies:
        copy.wait()


def body(tokens, norm_gain, w_qkv, w_out, bias_table, cotangent):
    nlon, nlat = lax.axis_size("lon"), lax.axis_size("lat")
    nz = nlon // 2
    width = tokens.shape[-1]
    rows = width // (nlon * nlat)
    half = CELLS // LEV
    vmem = pl.BlockSpec(memory_space=pltpu.VMEM)
    hbm = pl.BlockSpec(memory_space=pl.ANY)
    copies = 4 + 4 + 4 * (nlat - 1 + nz - 1 + 1) + 2 + 2 + 3 + 6
    shape = lambda *dims: pltpu.VMEM(dims, BF16)
    outs = (
        jax.ShapeDtypeStruct((LEV, half, width), BF16),
        jax.ShapeDtypeStruct((LEV, half, width), BF16),
        jax.ShapeDtypeStruct((rows, 768), F32),
    )
    results = pl.pallas_call(
        functools.partial(kernel, nlon, nlat),
        out_shape=outs + (jax.ShapeDtypeStruct((rows, 256), F32),),
        in_specs=[vmem] * 15,
        out_specs=(hbm, hbm, vmem, vmem),
        scratch_shapes=[
            shape(2, G_ROWS - 112, width),
            shape(2, G_ROWS, width),
            shape(CELLS, width),
            shape(CELLS, width),
            shape(CELLS, width),
            shape(width, CELLS),
            shape(width, CELLS),
            shape(CELLS, 768),
            shape(CELLS, 256),
            pltpu.VMEM((768, 128), F32),
            pltpu.VMEM((WINDOW, SEL), F32),
            pltpu.VMEM((4, WINDOW, WINDOW), F32),
            shape(CELLS, 768),
            shape(CELLS, 256),
            shape(4, 2, nz, nlat, rows, 256),
            shape(3, nlat - 1, 2, nz, rows, 256),
            shape(3, 2, nz, rows, 256),
            shape(max(nz - 1, 1), 2, nlat, rows, 256),
            shape(2, nlat, rows, 256),
            shape(3, max(nz - 1, 1), 2, rows, 256),
            shape(nlat - 1, 2, rows, 256),
            shape(4, 2, rows, 256),
            shape(4, rows, 256),
            shape(LEV, 2, T_ROWS, width),
            shape(2, T_ROWS, width),
            shape(T_ROWS, width),
            shape(T_ROWS, width),
            shape(T_ROWS, width),
            shape(U_ROWS, width),
            shape(U_ROWS, width),
            shape(2, LEV, T_ROWS, width),
            shape(2, LEV, half, width),
            pltpu.SemaphoreType.DMA((copies,)),
            pltpu.SemaphoreType.DMA((copies,)),
            pltpu.SemaphoreType.DMA((4,)),
        ],
        compiler_params=pltpu.CompilerParams(
            collective_id=0, has_side_effects=True, vmem_limit_bytes=56 * 1024 * 1024
        ),
    )(
        tokens.reshape(CELLS, width), cotangent.reshape(CELLS, width), norm_gain.reshape(1, width),
        w_qkv, w_out, bias_table, *[jnp.asarray(t) for t in tables()],
    )
    layer, dtok, gqkv, gout = pl.pallas_call(
        finisher,
        out_shape=outs + (jax.ShapeDtypeStruct((256, rows), F32),),
        in_specs=[hbm, hbm, hbm, vmem],
        out_specs=(hbm, hbm, hbm, vmem),
        scratch_shapes=[pltpu.VMEM((max(128, rows), 256), F32), pltpu.SemaphoreType.DMA((3,))],
    )(*results)
    field = (LEV, WLAT, LON, width)
    return layer.reshape(field), dtok.reshape(field), gqkv, gout


def solution(mesh):
    in_specs = (
        P(None, "lat", "lon", None),
        P(),
        P(None, "head"),
        P("head", None),
        P(None, "head"),
        P(None, "lat", "lon", None),
    )
    out_specs = (
        P(None, "lat", "lon", None),
        P(None, "lat", "lon", None),
        P(("lon", "lat"), "head"),
        P("head", ("lon", "lat")),
    )
    return jax.shard_map(body, mesh=mesh, in_specs=in_specs, out_specs=out_specs, check_vma=False)
```

time: 75.7 us -> 113 us (1.49)
  Pallas kernels: 69.5 us -> 109 us
  local copies, waits for them, and re-layouts: 5.35 us -> 3.22 us
    pallas_call x1 -> x2, Pallas kernels: 69.5 us -> 109 us  [the longest x1 69 us: body(): pl.pallas_call(functools.partial(kernel, nlon, nlat), out_shape=outs + (j...]
    pad x1 -> x0, local copies, waits for them, and re-layouts: 1.32 us -> none  [body(): table = jnp.pad(bias_table.T, ((0, 4), (0, 768 - bias_table.shape[0])))]
    unnamed x10 -> x2, local copies, waits for them, and re-layouts: 4.03 us -> 3.22 us
where the time goes in v2:
time: 113 us
  Pallas kernels  109 us (96%)
  local copies, waits for them, and re-layouts  3.22 us (3%)
    pallas_call x1, Pallas kernels, body(): pl.pallas_call(functools.partial(kernel, nlon, nlat), out_shape=outs + (j...  69 us
    pallas_call x1, Pallas kernels, body(): pl.pallas_call(finisher, out_shape=outs + (jax.ShapeDtypeStruct((256, row...  39.7 us
    unnamed x2, local copies, waits for them, and re-layouts  3.22 us

profile of v2, /device:TPU:1, one launch (start us, length us, event | category | flops | bytes accessed | tf_op | source)
XLA Modules:
  0.0 112.5 jit_solution(14934829947567800244)
XLA Ops:
  0.6 1.6 %copy.19.table_ref = f32[759,4]{1,0:T(8,128)} copy(f32[759,4]{0,1:T(4,128)} %param.19) | data formatting | bytes 24288 | tf_op args[4]
  2.3 69.0 %shard_map.174 = (bf16[2,144,1024]{2,1,0:T(8,128)(2,1)}, bf16[2,144,1024]{2,1,0:T(8,128)(2,1)}, f32[16,768]{1,0:T(8,128)}, f32[16,256]{1,0:T(8,128)}) custom-call(bf16[288,1024]{1,0:T(8,128)(2,1)} %bitcast.5, bf16[288,1024]{1,0:T(8,128)(2,1)} %bitcast.6, f32[1,1024]{1,0:T(1,128)} %bitcast.7, bf16[1024,768]{1,0:T(8,128)(2,1)} %wqkv_ref.1, ...), custom_call_target="tpu_custom_call" | custom-call | tf_op jit(solution)/shard_map/pallas_call | solution.py:396
  71.2 39.7 %shard_map.175 = (bf16[2,144,1024]{2,1,0:T(8,128)(2,1)}, bf16[2,144,1024]{2,1,0:T(8,128)(2,1)}, f32[16,768]{1,0:T(8,128)}, f32[256,16]{1,0:T(8,128)}) custom-call(bf16[2,144,1024]{2,1,0:T(8,128)(2,1)} %get-tuple-element.12.layer_in, bf16[2,144,1024]{2,1,0:T(8,128)(2,1)} %get-tuple-element.13.dtok_in, f32[16,768]{1,0:T(8,128)} %get-tuple-element.14.gqkv_in, ...), custom_call_target="tpu_custom_call" | custom-call | tf_op jit(solution)/shard_map/pallas_call | solution.py:445
  111.0 1.6 %copy.20 = f32[256,16]{0,1:T(8,128)} copy(f32[256,16]{1,0:T(8,128)} %get-tuple-element.23) | data formatting | bytes 32768

commit v3 on v2

--- a/solution.py
+++ b/solution.py
@@ -24,9 +24,9 @@
 
 G_START = (0, 112, 224, 272)
 G_ROWS = 320
-T_START = (96, 0, 54, 72)
+T_START = (90, 0, 54, 72)
 T_AWAY = 96
-T_ROWS = 160
+T_ROWS = 144
 U_START = (None, 0, 64, 96)
 U_ROWS = 128
 SEL = 384
@@ -44,6 +44,7 @@
     compact = np.zeros((CELLS, G_ROWS), np.float32)
     level = np.zeros((LEV, T_ROWS, CELLS), np.float32)
     spread = np.zeros((U_ROWS, T_AWAY), np.float32)
+    gather = np.zeros((T_AWAY, U_ROWS + T_AWAY), np.float32)
     natural = np.zeros((CELLS // LEV, T_ROWS), np.float32)
     for lv in range(LEV):
         for row in range(WLAT):
@@ -60,12 +61,15 @@
                     natural[src_row * LON + src_col, T_START[part] + index] = 1
                     if part:
                         spread[U_START[part] + index, T_START[part] + index] = 1
+                        gather[T_START[part] + index, U_START[part] + index] = 1
+                    elif index < 6:
+                        gather[T_START[part] + index, U_ROWS + T_START[part] + index] = 1
     select = np.zeros((SEL, WINDOW), np.float32)
     for i in range(WINDOW):
         select[(i // 72) * 253 + (i // WLON % WLAT) * 23 + i % WLON, i] = 1
     half = np.arange(WINDOW) // WLON % WLAT >= 3
     cross = (half[:, None] != half[None, :]).astype(np.float32)
-    exact = [t.astype(ml_dtypes.bfloat16) for t in (own, compact, level, spread, spread.T, natural, select, np.eye(128, dtype=np.float32))]
+    exact = [t.astype(ml_dtypes.bfloat16) for t in (own, compact, level, spread, gather, natural, select, np.eye(128, dtype=np.float32))]
     return exact + [cross]
 
 
@@ -81,13 +85,15 @@
 
 def kernel(
     nlon, nlat,
-    tok_ref, cot_ref, gain_ref, wqkv_ref, wout_ref, table_ref,
-    own_ref, compact_ref, level_ref, spread_ref, gather_ref, natural_ref, select_ref, eye_ref, cross_ref,
-    layer_ref, dtok_ref, gqkv_ref, gout_ref,
+    tok_in, cot_in, own_in, table_in, select_in, cross_in, compact_in, gain_in, wqkv_in, wout_in, eye_in,
+    level_in, spread_in, gather_in, natural_in,
+    field_ref, gqkv_ref, gout_ref,
     sent, held, tokc, cotc, normed, normed_t, cot_t, qkv, datt, wide_table, rolled, bias, dqkv, att,
     wgt, near_x, sum_x, near_z, first_z, sum_z, last_x, sum_y, from_y,
-    term, from_core, to_side, from_side, result, spread_out, back, final, fields,
-    send_sem, recv_sem, out_sem,
+    term, from_core, to_side, from_side, result, spread_out, back, final,
+    tok_ref, cot_ref, own_ref, table_ref, select_ref, cross_ref, compact_ref, gain_ref, wqkv_ref, wout_ref, eye_ref,
+    level_ref, spread_ref, gather_ref, natural_ref,
+    send_sem, recv_sem, in_sem,
 ):
     lon, lat, head = lax.axis_index("lon"), lax.axis_index("lat"), lax.axis_index("head")
     nz = nlon // 2
@@ -112,6 +118,19 @@
     for source in sources:
         pl.semaphore_signal(barrier, inc=1, device_id=source, device_id_type=MESH)
 
+    loads = [
+        pltpu.make_async_copy(src, dst, in_sem.at[i])
+        for i, (src, dst) in enumerate((
+            (tok_in, tok_ref), (cot_in, cot_ref), (own_in, own_ref), (table_in, table_ref), (select_in, select_ref),
+            (cross_in, cross_ref), (compact_in, compact_ref), (gain_in, gain_ref), (wqkv_in, wqkv_ref), (wout_in, wout_ref),
+            (eye_in, eye_ref), (level_in, level_ref), (spread_in, spread_ref), (gather_in, gather_ref), (natural_in, natural_ref),
+        ))
+    ]
+    for load in loads:
+        load.start()
+    for load in loads[:3]:
+        load.wait()
+
     count = [0]
 
     def remote(src, dst, target):
@@ -141,9 +160,12 @@
         remote(sent.at[core, pl.ds(at - 112, size)], held.at[core, pl.ds(at, size)], target) for at, size, target in parts
     ])
 
+    for load in loads[3:]:
+        load.wait()
+
     wide_table[...] = jnp.zeros(wide_table.shape, F32)
-    wide_table[0 : table_ref.shape[0], 0:4] = table_ref[...]
-    turned = wide_table[...].T
+    wide_table[0:4, 0 : table_ref.shape[1]] = table_ref[...]
+    turned = wide_table[...]
     for h in range(4):
         stepped = jnp.broadcast_to(turned[h : h + 1, :], (16, turned.shape[1]))
         stepped = pltpu.roll(stepped, 0, 1, stride=1, stride_axis=0)
@@ -206,6 +228,8 @@
         wgt[h, :, :, :, :, 0:192] = wide.reshape(2, nz, nlat, rows_out, 192)
         narrow = dot(cot_t[...], att[:, 64 * h : 64 * h + 64]).astype(BF16)
         wgt[h, :, :, :, :, 192:256] = narrow.reshape(2, nz, nlat, rows_out, 64)
+
+    def leave(h):
         if h == 0:
             on_first[h] = start([
                 remote(wgt.at[h, :, target["lon"] - y_hi * nz], near_z.at[d], target) for d, target in enumerate(z_up)
@@ -260,6 +284,7 @@
             attend(w, h)
         if h < 3:
             weight(h)
+            leave(h)
 
     chunks = ((0, T_AWAY), (T_AWAY, T_ROWS - T_AWAY))
     on_core = []
@@ -314,66 +339,59 @@
         copy.wait_recv()
         return start([remote(final.at[1 - kind, core, rows], final.at[1 - kind, core, rows], sibling)])[0]
 
-    outs = []
-
     def place(k, lv):
-        fields[k, lv] = dot(natural_ref[...], final[k, lv]).astype(BF16)
-        for index, ref in enumerate((layer_ref, dtok_ref)):
-            @pl.when(k == index)
-            def _():
-                pltpu.make_async_copy(fields.at[k, lv], ref.at[lv], out_sem.at[len(outs)]).start()
-        outs.append(pltpu.make_async_copy(fields.at[k, lv], layer_ref.at[lv], out_sem.at[len(outs)]))
-
+        field_ref[k, lv] = dot(natural_ref[...], final[k, lv]).astype(BF16)
+
+    second(1)
     finish(0)
     spread_out[...] = dot(spread_ref[...], result[0:T_AWAY]).astype(BF16)
     returned = start([
         remote(spread_out.at[pl.ds(at, size)], back.at[pl.ds(at, size)], target)
         for at, size, target in ((0, 64, {"lat": lat_up}), (64, 32, {"lon": lon_up}), (96, 32, {"lat": lat_up, "lon": lon_up}))
     ])
+    leave(3)
     finish(1)
     final[kind, core, T_AWAY:T_ROWS] = result[T_AWAY:T_ROWS]
     shared = [share(1)]
-    second(1)
+    second(0)
+    second(2)
+    third(1)
+    relayed = [relay(1, shared[0][0])]
     for copy in returned:
         copy.wait_recv()
+    back[U_ROWS : U_ROWS + T_AWAY] = result[0:T_AWAY]
     final[kind, core, 0:T_AWAY] = dot(gather_ref[...], back[...]).astype(BF16)
     shared = [share(0)] + shared
     place(kind, core)
-    second(0)
-    relayed = [relay(1, shared[1][0])]
-    second(2)
-    third(1)
+    third(2)
+    third(0)
+    second(3)
     relayed.append(relay(0, shared[0][0]))
     place(1 - kind, core)
+    last(1)
     for _, copy in shared:
         copy.wait_recv()
     place(kind, 1 - core)
-    third(0)
+    third(3)
     for copy in relayed:
         copy.wait_recv()
     place(1 - kind, 1 - core)
-    second(3)
-    third(2)
-    last(1)
     last(0)
-    third(3)
     last(2)
     last(3)
     for copy in started:
         copy.wait_send()
-    for copy in outs:
-        copy.wait()
-
-
-def finisher(layer_in, dtok_in, gqkv_in, gout_in, layer_out, dtok_out, gqkv_out, gout_out, turned, sem):
+
+
+def finisher(fields, gqkv_in, gout_in, layer_out, dtok_out, gqkv_out, gout_out, sem):
     copies = [
         pltpu.make_async_copy(src, dst, sem.at[i])
-        for i, (src, dst) in enumerate(((layer_in, layer_out), (dtok_in, dtok_out), (gqkv_in, gqkv_out)))
+        for i, (src, dst) in enumerate((
+            (fields.at[0], layer_out), (fields.at[1], dtok_out), (gqkv_in, gqkv_out), (gout_in, gout_out),
+        ))
     ]
     for copy in copies:
         copy.start()
-    turned[0 : gout_in.shape[0], :] = gout_in[...]
-    gout_out[...] = turned[...].T[:, 0 : gout_in.shape[0]]
     for copy in copies:
         copy.wait()
 
@@ -392,12 +410,18 @@
         jax.ShapeDtypeStruct((LEV, half, width), BF16),
         jax.ShapeDtypeStruct((LEV, half, width), BF16),
         jax.ShapeDtypeStruct((rows, 768), F32),
+        jax.ShapeDtypeStruct((rows, 256), F32),
+    )
+    own, compact, level, spread, gather, natural, select, eye, cross = [jnp.asarray(t) for t in tables()]
+    operands = (
+        tokens.reshape(CELLS, width), cotangent.reshape(CELLS, width), own, bias_table.T, select, cross, compact,
+        norm_gain.reshape(1, width), w_qkv, w_out, eye, level, spread, gather, natural,
     )
     results = pl.pallas_call(
         functools.partial(kernel, nlon, nlat),
-        out_shape=outs + (jax.ShapeDtypeStruct((rows, 256), F32),),
-        in_specs=[vmem] * 15,
-        out_specs=(hbm, hbm, vmem, vmem),
+        out_shape=(pltpu.VMEM((2, LEV, half, width), BF16), pltpu.VMEM((rows, 768), F32), pltpu.VMEM((rows, 256), F32)),
+        in_specs=[hbm] * 15,
+        out_specs=(vmem, vmem, vmem),
         scratch_shapes=[
             shape(2, G_ROWS - 112, width),
             shape(2, G_ROWS, width),
@@ -408,7 +432,7 @@
             shape(width, CELLS),
             shape(CELLS, 768),
             shape(CELLS, 256),
-            pltpu.VMEM((768, 128), F32),
+            pltpu.VMEM((8, 768), F32),
             pltpu.VMEM((WINDOW, SEL), F32),
             pltpu.VMEM((4, WINDOW, WINDOW), F32),
             shape(CELLS, 768),
@@ -428,29 +452,26 @@
             shape(T_ROWS, width),
             shape(T_ROWS, width),
             shape(U_ROWS, width),
-            shape(U_ROWS, width),
+            shape(U_ROWS + T_AWAY, width),
             shape(2, LEV, T_ROWS, width),
-            shape(2, LEV, half, width),
+            *[pltpu.VMEM(x.shape, x.dtype) for x in operands],
             pltpu.SemaphoreType.DMA((copies,)),
             pltpu.SemaphoreType.DMA((copies,)),
-            pltpu.SemaphoreType.DMA((4,)),
+            pltpu.SemaphoreType.DMA((len(operands),)),
         ],
         compiler_params=pltpu.CompilerParams(
             collective_id=0, has_side_effects=True, vmem_limit_bytes=56 * 1024 * 1024
         ),
-    )(
-        tokens.reshape(CELLS, width), cotangent.reshape(CELLS, width), norm_gain.reshape(1, width),
-        w_qkv, w_out, bias_table, *[jnp.asarray(t) for t in tables()],
-    )
+    )(*operands)
     layer, dtok, gqkv, gout = pl.pallas_call(
         finisher,
-        out_shape=outs + (jax.ShapeDtypeStruct((256, rows), F32),),
-        in_specs=[hbm, hbm, hbm, vmem],
-        out_specs=(hbm, hbm, hbm, vmem),
-        scratch_shapes=[pltpu.VMEM((max(128, rows), 256), F32), pltpu.SemaphoreType.DMA((3,))],
+        out_shape=outs,
+        in_specs=[vmem] * 3,
+        out_specs=(hbm,) * 4,
+        scratch_shapes=[pltpu.SemaphoreType.DMA((4,))],
     )(*results)
     field = (LEV, WLAT, LON, width)
-    return layer.reshape(field), dtok.reshape(field), gqkv, gout
+    return layer.reshape(field), dtok.reshape(field), gqkv, gout.T
 
 
 def solution(mesh):

time: 113 us -> 66.2 us (0.59)
  Pallas kernels: 109 us -> 62.5 us
    pallas_call x2, Pallas kernels: 109 us -> 62.5 us  [the longest x1 60.2 us: body(): pl.pallas_call(functools.partial(kernel, nlon, nlat), out_shape=(pltpu.VM...]
    unnamed x2 -> x6, local copies, waits for them, and re-layouts: 3.22 us -> 2.22 us
where the time goes in v3:
time: 66.2 us; the launch traced here: 65.4 us
  Pallas kernels  62.5 us (94%)
  local copies, waits for them, and re-layouts  2.22 us (3%)
    pallas_call x1, Pallas kernels, body(): pl.pallas_call(functools.partial(kernel, nlon, nlat), out_shape=(pltpu.VM...  60.2 us
    pallas_call x1, Pallas kernels, body(): pl.pallas_call(finisher, out_shape=outs, in_specs=[vmem] * 3, out_specs=(...  2.35 us
    unnamed x6, local copies, waits for them, and re-layouts  2.22 us

profile of v3, /device:TPU:1, one launch (start us, length us, event | category | flops | bytes accessed | tf_op | source)
XLA Modules:
  0.0 65.4 jit_solution(17340396507431809633)
XLA Ops:
  0.6 60.2 %shard_map.174 = (bf16[2,2,144,1024]{3,2,1,0:T(8,128)(2,1)S(1)}, f32[16,768]{1,0:T(8,128)S(1)}, f32[16,256]{1,0:T(8,128)S(1)}) custom-call(bf16[288,1024]{1,0:T(8,128)(2,1)} %bitcast.7, bf16[288,1024]{1,0:T(8,128)(2,1)} %bitcast.8, bf16[320,288]{1,0:T(8,128)(2,1)} %constant.18.clone.own_in, f32[4,759]{1,0:T(4,128)} %bitcast.9, ...), custom_call_target="tpu_custom_call" | custom-call | tf_op jit(solution)/shard_map/pallas_call | solution.py:420
  60.8 0.0 copy-start
  60.8 1.0 %copy-done = bf16[2,2,144,1024]{3,2,1,0:T(8,128)(2,1)} copy-done((bf16[2,2,144,1024]{3,2,1,0:T(8,128)(2,1)}, bf16[2,2,144,1024]{3,2,1,0:T(8,128)(2,1)S(1)}, u32[]{:S(2)}) %copy-start) | copy-done | bytes 1179672
  61.8 0.0 copy-start.1
  61.8 0.6 copy-done.1
  62.4 0.0 copy-start.2
  62.4 0.6 copy-done.2
  63.0 2.3 %shard_map.175 = (bf16[2,144,1024]{2,1,0:T(8,128)(2,1)}, bf16[2,144,1024]{2,1,0:T(8,128)(2,1)}, f32[16,768]{1,0:T(8,128)}, f32[16,256]{1,0:T(8,128)}) custom-call(bf16[2,2,144,1024]{3,2,1,0:T(8,128)(2,1)} %copy-done, f32[16,768]{1,0:T(8,128)} %copy-done.1, f32[16,256]{1,0:T(8,128)} %copy-done.2), custom_call_target="tpu_custom_call" | custom-call | tf_op jit(solution)/shard_map/pallas_call | solution.py:466
Async XLA Ops:
  60.8 1.0 %copy-start = (bf16[2,2,144,1024]{3,2,1,0:T(8,128)(2,1)}, bf16[2,2,144,1024]{3,2,1,0:T(8,128)(2,1)S(1)}, u32[]{:S(2)}) copy-start(bf16[2,2,144,1024]{3,2,1,0:T(8,128)(2,1)S(1)} %get-tuple-element.11.fields) | copy-start | bytes 3538948
  61.8 0.6 copy-start.1
  62.4 0.6 copy-start.2

commit v4 on v3

--- a/solution.py
+++ b/solution.py
@@ -25,10 +25,10 @@
 G_START = (0, 112, 224, 272)
 G_ROWS = 320
 T_START = (90, 0, 54, 72)
-T_AWAY = 96
 T_ROWS = 144
-U_START = (None, 0, 64, 96)
-U_ROWS = 128
+CHUNK = 48
+U_START = (None, 0, 16, 48)
+U_ROWS = 80
 SEL = 384
 
 
@@ -43,8 +43,8 @@
     own = np.zeros((G_ROWS, CELLS), np.float32)
     compact = np.zeros((CELLS, G_ROWS), np.float32)
     level = np.zeros((LEV, T_ROWS, CELLS), np.float32)
-    spread = np.zeros((U_ROWS, T_AWAY), np.float32)
-    gather = np.zeros((T_AWAY, U_ROWS + T_AWAY), np.float32)
+    spread = np.zeros((U_ROWS, CHUNK), np.float32)
+    gather = np.zeros((CHUNK, U_ROWS + CHUNK), np.float32)
     natural = np.zeros((CELLS // LEV, T_ROWS), np.float32)
     for lv in range(LEV):
         for row in range(WLAT):
@@ -59,11 +59,13 @@
                 level[lv, T_START[part] + index, place] = 1
                 if lv == 0:
                     natural[src_row * LON + src_col, T_START[part] + index] = 1
-                    if part:
-                        spread[U_START[part] + index, T_START[part] + index] = 1
-                        gather[T_START[part] + index, U_START[part] + index] = 1
-                    elif index < 6:
-                        gather[T_START[part] + index, U_ROWS + T_START[part] + index] = 1
+                    at = T_START[part] + index - CHUNK
+                    if 0 <= at < CHUNK and part:
+                        travel = U_START[part] + (at if part == 1 else index)
+                        spread[travel, at] = 1
+                        gather[at, travel] = 1
+                    elif 0 <= at < CHUNK:
+                        gather[at, U_ROWS + at] = 1
     select = np.zeros((SEL, WINDOW), np.float32)
     for i in range(WINDOW):
         select[(i // 72) * 253 + (i // WLON % WLAT) * 23 + i % WLON, i] = 1
@@ -87,10 +89,10 @@
     nlon, nlat,
     tok_in, cot_in, own_in, table_in, select_in, cross_in, compact_in, gain_in, wqkv_in, wout_in, eye_in,
     level_in, spread_in, gather_in, natural_in,
-    field_ref, gqkv_ref, gout_ref,
+    layer_ref, dtok_ref, gqkv_ref, gout_ref,
     sent, held, tokc, cotc, normed, normed_t, cot_t, qkv, datt, wide_table, rolled, bias, dqkv, att,
     wgt, near_x, sum_x, near_z, first_z, sum_z, last_x, sum_y, from_y,
-    term, from_core, to_side, from_side, result, spread_out, back, final,
+    term, from_core, to_side, from_side, tok_l, cot_l, result, spread_out, back, final,
     tok_ref, cot_ref, own_ref, table_ref, select_ref, cross_ref, compact_ref, gain_ref, wqkv_ref, wout_ref, eye_ref,
     level_ref, spread_ref, gather_ref, natural_ref,
     send_sem, recv_sem, in_sem,
@@ -286,19 +288,18 @@
             weight(h)
             leave(h)
 
-    chunks = ((0, T_AWAY), (T_AWAY, T_ROWS - T_AWAY))
-    on_core = []
-    for lv in (1 - core, core):
-        for at, size in chunks:
-            order = level_ref[lv, at : at + size]
-            att_l = dot(order, att[...]).astype(BF16)
-            dqkv_l = dot(order, dqkv[...]).astype(BF16)
-            term[lv, 0, at : at + size] = dot(att_l, wout_ref[...]).astype(BF16)
-            term[lv, 1, at : at + size] = dot(dqkv_l, wqkv_ref[...], 1, 1).astype(BF16)
-            if lv is not core:
-                on_core += start([
-                    remote(term.at[1 - core, :, pl.ds(at, size)], from_core.at[:, pl.ds(at, size)], sibling)
-                ])
+    def sum_heads(lv):
+        att_l = dot(level_ref[lv], att[...]).astype(BF16)
+        dqkv_l = dot(level_ref[lv], dqkv[...]).astype(BF16)
+        term[lv, 0] = dot(att_l, wout_ref[...]).astype(BF16)
+        term[lv, 1] = dot(dqkv_l, wqkv_ref[...], 1, 1).astype(BF16)
+
+    chunks = [(at, CHUNK) for at in range(0, T_ROWS, CHUNK)]
+    sum_heads(1 - core)
+    on_core = start([
+        remote(term.at[1 - core, :, pl.ds(at, size)], from_core.at[:, pl.ds(at, size)], sibling) for at, size in chunks
+    ])
+    sum_heads(core)
     on_side = []
     for copy, (at, size) in zip(on_core, chunks):
         copy.wait_recv()
@@ -306,26 +307,25 @@
         to_side[rows] = (term[core, 1 - kind, rows].astype(F32) + from_core[1 - kind, rows].astype(F32)).astype(BF16)
         on_side += start([remote(to_side.at[rows], from_side.at[rows], side)])
     weight(3)
+    tok_l[...] = dot(level_ref[core], tokc[...])
+    cot_l[...] = dot(level_ref[core], cotc[...])
 
     def finish(chunk):
-        at, size = chunks[chunk]
-        rows = pl.ds(at, size)
-        tok_l = dot(level_ref[core, at : at + size], tokc[...])
-        cot_l = dot(level_ref[core, at : at + size], cotc[...])
+        rows = pl.ds(*chunks[chunk])
         on_side[chunk].wait_recv()
         total = term[core, kind, rows].astype(F32) + from_core[kind, rows].astype(F32) + from_side[rows].astype(F32)
 
         @pl.when(kind == 0)
         def _():
-            result[rows] = (tok_l + total).astype(BF16)
+            result[rows] = (tok_l[rows] + total).astype(BF16)
 
         @pl.when(kind == 1)
         def _():
-            scaled, inverse = layer_norm(tok_l)
+            scaled, inverse = layer_norm(tok_l[rows])
             grad = total * gain_ref[...]
             mean_grad = jnp.mean(grad, axis=-1, keepdims=True)
             mean_mixed = jnp.mean(grad * scaled, axis=-1, keepdims=True)
-            result[rows] = (cot_l + (grad - mean_grad - scaled * mean_mixed) * inverse).astype(BF16)
+            result[rows] = (cot_l[rows] + (grad - mean_grad - scaled * mean_mixed) * inverse).astype(BF16)
 
     def share(chunk):
         rows = pl.ds(*chunks[chunk])
@@ -340,37 +340,50 @@
         return start([remote(final.at[1 - kind, core, rows], final.at[1 - kind, core, rows], sibling)])[0]
 
     def place(k, lv):
-        field_ref[k, lv] = dot(natural_ref[...], final[k, lv]).astype(BF16)
-
+        field = dot(natural_ref[...], final[k, lv]).astype(BF16)
+
+        @pl.when(k == 0)
+        def _():
+            layer_ref[lv] = field
+
+        @pl.when(k == 1)
+        def _():
+            dtok_ref[lv] = field
+
+    first, middle, end = (pl.ds(*chunk) for chunk in chunks)
+    finish(0)
+    straight = start([remote(result.at[first], final.at[kind, core, first], {"lat": lat_up})])[0]
     second(1)
-    finish(0)
-    spread_out[...] = dot(spread_ref[...], result[0:T_AWAY]).astype(BF16)
+    finish(1)
+    spread_out[...] = dot(spread_ref[...], result[middle]).astype(BF16)
     returned = start([
         remote(spread_out.at[pl.ds(at, size)], back.at[pl.ds(at, size)], target)
-        for at, size, target in ((0, 64, {"lat": lat_up}), (64, 32, {"lon": lon_up}), (96, 32, {"lat": lat_up, "lon": lon_up}))
+        for at, size, target in ((0, 16, {"lat": lat_up}), (16, 32, {"lon": lon_up}), (48, 32, {"lat": lat_up, "lon": lon_up}))
     ])
     leave(3)
-    finish(1)
-    final[kind, core, T_AWAY:T_ROWS] = result[T_AWAY:T_ROWS]
-    shared = [share(1)]
+    finish(2)
+    final[kind, core, end] = result[end]
+    shared = {2: share(2)}
+    straight.wait_recv()
+    shared[0] = share(0)
     second(0)
     second(2)
     third(1)
-    relayed = [relay(1, shared[0][0])]
     for copy in returned:
         copy.wait_recv()
-    back[U_ROWS : U_ROWS + T_AWAY] = result[0:T_AWAY]
-    final[kind, core, 0:T_AWAY] = dot(gather_ref[...], back[...]).astype(BF16)
-    shared = [share(0)] + shared
+    back[U_ROWS : U_ROWS + CHUNK] = result[middle]
+    final[kind, core, middle] = dot(gather_ref[...], back[...]).astype(BF16)
+    shared[1] = share(1)
     place(kind, core)
+    relayed = [relay(2, shared[2][0]), relay(0, shared[0][0])]
     third(2)
     third(0)
     second(3)
-    relayed.append(relay(0, shared[0][0]))
+    relayed.append(relay(1, shared[1][0]))
     place(1 - kind, core)
     last(1)
-    for _, copy in shared:
-        copy.wait_recv()
+    for chunk in range(3):
+        shared[chunk][1].wait_recv()
     place(kind, 1 - core)
     third(3)
     for copy in relayed:
@@ -381,19 +394,6 @@
     last(3)
     for copy in started:
         copy.wait_send()
-
-
-def finisher(fields, gqkv_in, gout_in, layer_out, dtok_out, gqkv_out, gout_out, sem):
-    copies = [
-        pltpu.make_async_copy(src, dst, sem.at[i])
-        for i, (src, dst) in enumerate((
-            (fields.at[0], layer_out), (fields.at[1], dtok_out), (gqkv_in, gqkv_out), (gout_in, gout_out),
-        ))
-    ]
-    for copy in copies:
-        copy.start()
-    for copy in copies:
-        copy.wait()
 
 
 def body(tokens, norm_gain, w_qkv, w_out, bias_table, cotangent):
@@ -404,24 +404,18 @@
     half = CELLS // LEV
     vmem = pl.BlockSpec(memory_space=pltpu.VMEM)
     hbm = pl.BlockSpec(memory_space=pl.ANY)
-    copies = 4 + 4 + 4 * (nlat - 1 + nz - 1 + 1) + 2 + 2 + 3 + 6
+    copies = 4 + 4 + 4 * (nlat - 1 + nz - 1 + 1) + 3 + 3 + 4 + 9
     shape = lambda *dims: pltpu.VMEM(dims, BF16)
-    outs = (
-        jax.ShapeDtypeStruct((LEV, half, width), BF16),
-        jax.ShapeDtypeStruct((LEV, half, width), BF16),
-        jax.ShapeDtypeStruct((rows, 768), F32),
-        jax.ShapeDtypeStruct((rows, 256), F32),
-    )
     own, compact, level, spread, gather, natural, select, eye, cross = [jnp.asarray(t) for t in tables()]
     operands = (
         tokens.reshape(CELLS, width), cotangent.reshape(CELLS, width), own, bias_table.T, select, cross, compact,
         norm_gain.reshape(1, width), w_qkv, w_out, eye, level, spread, gather, natural,
     )
-    results = pl.pallas_call(
+    layer, dtok, gqkv, gout = pl.pallas_call(
         functools.partial(kernel, nlon, nlat),
-        out_shape=(pltpu.VMEM((2, LEV, half, width), BF16), pltpu.VMEM((rows, 768), F32), pltpu.VMEM((rows, 256), F32)),
+        out_shape=(shape(LEV, half, width), shape(LEV, half, width), pltpu.VMEM((rows, 768), F32), pltpu.VMEM((rows, 256), F32)),
         in_specs=[hbm] * 15,
-        out_specs=(vmem, vmem, vmem),
+        out_specs=(vmem,) * 4,
         scratch_shapes=[
             shape(2, G_ROWS - 112, width),
             shape(2, G_ROWS, width),
@@ -450,9 +444,11 @@
             shape(2, T_ROWS, width),
             shape(T_ROWS, width),
             shape(T_ROWS, width),
+            pltpu.VMEM((T_ROWS, width), F32),
+            pltpu.VMEM((T_ROWS, width), F32),
             shape(T_ROWS, width),
             shape(U_ROWS, width),
-            shape(U_ROWS + T_AWAY, width),
+            shape(U_ROWS + CHUNK, width),
             shape(2, LEV, T_ROWS, width),
             *[pltpu.VMEM(x.shape, x.dtype) for x in operands],
             pltpu.SemaphoreType.DMA((copies,)),
@@ -463,13 +459,6 @@
             collective_id=0, has_side_effects=True, vmem_limit_bytes=56 * 1024 * 1024
         ),
     )(*operands)
-    layer, dtok, gqkv, gout = pl.pallas_call(
-        finisher,
-        out_shape=outs,
-        in_specs=[vmem] * 3,
-        out_specs=(hbm,) * 4,
-        scratch_shapes=[pltpu.SemaphoreType.DMA((4,))],
-    )(*results)
     field = (LEV, WLAT, LON, width)
     return layer.reshape(field), dtok.reshape(field), gqkv, gout.T
 

time: 66.2 us -> 62.7 us (0.947)
  Pallas kernels: 62.5 us -> 58.6 us
    pallas_call x2 -> x1, Pallas kernels: 62.5 us -> 58.6 us  [body(): pl.pallas_call(functools.partial(kernel, nlon, nlat), out_shape=(shape(LE...]
    unnamed x6 -> x4, local copies, waits for them, and re-layouts: 2.22 us -> 2.86 us
where the time goes in v4:
time: 62.7 us; the launch traced here: 62.1 us
  Pallas kernels  58.6 us (93%)
  local copies, waits for them, and re-layouts  2.86 us (5%)
  between operations  0.64 us (1%)
    pallas_call x1, Pallas kernels, body(): pl.pallas_call(functools.partial(kernel, nlon, nlat), out_shape=(shape(LE...  58.6 us
    unnamed x4, local copies, waits for them, and re-layouts  2.86 us

profile of v4, /device:TPU:1, one launch (start us, length us, event | category | flops | bytes accessed | tf_op | source)
XLA Modules:
  0.0 62.1 jit_solution(10087663083134248324)
XLA Ops:
  0.6 58.6 %shard_map.174 = (bf16[2,144,1024]{2,1,0:T(8,128)(2,1)S(1)}, bf16[2,144,1024]{2,1,0:T(8,128)(2,1)S(1)}, f32[16,768]{1,0:T(8,128)S(1)}, f32[16,256]{1,0:T(8,128)S(1)}) custom-call(bf16[288,1024]{1,0:T(8,128)(2,1)} %bitcast.10, bf16[288,1024]{1,0:T(8,128)(2,1)} %bitcast.11, bf16[320,288]{1,0:T(8,128)(2,1)} %constant.18.clone.own_in, f32[4,759]{1,0:T(4,128)} %bitcast.12, ...), custom_call_target="tpu_custom_call" | custom-call | tf_op jit(solution)/shard_map/pallas_call | solution.py:414
  59.3 0.8 %copy.23 = bf16[2,6,24,1024]{3,2,1,0:T(8,128)(2,1)} copy(bf16[2,6,24,1024]{3,2,1,0:T(8,128)(2,1)S(1)} %bitcast.8) | data formatting | bytes 1179648
  60.1 0.8 %copy.24 = bf16[2,6,24,1024]{3,2,1,0:T(8,128)(2,1)} copy(bf16[2,6,24,1024]{3,2,1,0:T(8,128)(2,1)S(1)} %bitcast.7) | data formatting | bytes 1179648
  60.9 0.6 copy.26
  61.5 0.6 copy.25

commit v5 on v4

--- a/solution.py
+++ b/solution.py
@@ -91,7 +91,8 @@
     level_in, spread_in, gather_in, natural_in,
     layer_ref, dtok_ref, gqkv_ref, gout_ref,
     sent, held, tokc, cotc, normed, normed_t, cot_t, qkv, datt, wide_table, rolled, bias, dqkv, att,
-    wgt, near_x, sum_x, near_z, first_z, sum_z, last_x, sum_y, from_y,
+    wgt, relay_up, relay_down, added_up, added_down, from_below, from_above, sum_x, from_lon,
+    near_z, first_z, last_x, sum_y, from_y,
     term, from_core, to_side, from_side, tok_l, cot_l, result, spread_out, back, final,
     tok_ref, cot_ref, own_ref, table_ref, select_ref, cross_ref, compact_ref, gain_ref, wqkv_ref, wout_ref, eye_ref,
     level_ref, spread_ref, gather_ref, natural_ref,
@@ -111,9 +112,11 @@
     z_down = [{"lon": y_hi * nz + (z + nz - d) % nz} for d in range(1, nz)]
     far = {"lon": (1 - y_hi) * nz + z}
 
-    sources = x_down + z_down + [
-        far, sibling, side,
-        {"lon": lon_up}, {"lon": lon_down},
+    lon_others = [{"lon": (lon + d) % nlon} for d in range(1, nlon)]
+    opposite = (lat + 2) % nlat
+
+    sources = x_down + lon_others + [
+        sibling, side,
         {"lat": lat_up, "lon": lon_up}, {"lat": lat_down, "lon": lon_down},
     ]
     barrier = pltpu.get_barrier_semaphore()
@@ -223,7 +226,8 @@
         dqkv[rows, first + 128 : first + 192] = dot(half, grad, 1, 0).astype(BF16)
 
     rows_out = wgt.shape[4]
-    on_first, on_second, on_y = {}, {}, {}
+    on_relay, on_first, on_second, on_y = {}, {}, {}, {}
+    low, high = pl.ds(0, 128), pl.ds(128, 128)
 
     def weight(h):
         wide = dot(normed_t[...], dqkv[:, 192 * h : 192 * h + 192]).astype(BF16)
@@ -237,9 +241,26 @@
                 remote(wgt.at[h, :, target["lon"] - y_hi * nz], near_z.at[d], target) for d, target in enumerate(z_up)
             ])
         else:
+            up, down = {"lat": lat_up}, {"lat": lat_down}
+            on_relay[h] = start([
+                remote(wgt.at[h, :, :, opposite, :, low], relay_up.at[h - 1], up),
+                remote(wgt.at[h, :, :, opposite, :, high], relay_down.at[h - 1], down),
+            ])
             on_first[h] = start([
-                remote(wgt.at[h, :, :, target["lat"]], near_x.at[h - 1, d], target) for d, target in enumerate(x_up)
+                remote(wgt.at[h, :, :, lat_up, :, high], from_below.at[h - 1, :, :, :, high], up),
+                remote(wgt.at[h, :, :, lat_down, :, low], from_above.at[h - 1, :, :, :, low], down),
             ])
+
+    def onward(h):
+        up, down = {"lat": lat_up}, {"lat": lat_down}
+        for copy in on_relay[h]:
+            copy.wait_recv()
+        added_up[h - 1] = (wgt[h, :, :, lat_up, :, low].astype(F32) + relay_up[h - 1].astype(F32)).astype(BF16)
+        added_down[h - 1] = (wgt[h, :, :, lat_down, :, high].astype(F32) + relay_down[h - 1].astype(F32)).astype(BF16)
+        on_first[h] += start([
+            remote(added_up.at[h - 1], from_below.at[h - 1, :, :, :, low], up),
+            remote(added_down.at[h - 1], from_above.at[h - 1, :, :, :, high], down),
+        ])
 
     def second(h):
         for copy in on_first[h]:
@@ -253,31 +274,31 @@
                 remote(first_z.at[:, target["lat"]], last_x.at[d], target) for d, target in enumerate(x_up)
             ])
         else:
-            total = wgt[h, :, :, lat].astype(F32)
-            for d in range(nlat - 1):
-                total = total + near_x[h - 1, d].astype(F32)
-            sum_x[h - 1] = total.astype(BF16)
+            total = wgt[h, :, :, lat].astype(F32) + from_below[h - 1].astype(F32) + from_above[h - 1].astype(F32)
+            sum_x[h - 1] = total.astype(BF16).reshape(sum_x.shape[1:])
             on_second[h] = start([
-                remote(sum_x.at[h - 1, :, target["lon"] - y_hi * nz], sum_z.at[h - 1, d], target) for d, target in enumerate(z_up)
+                remote(sum_x.at[h - 1, target["lon"]], from_lon.at[h - 1, d], target) for d, target in enumerate(lon_others)
             ])
 
     def third(h):
         for copy in on_second[h]:
             copy.wait_recv()
+        total = first_z[:, lat].astype(F32)
+        for d in range(nlat - 1):
+            total = total + last_x[d].astype(F32)
+        sum_y[...] = total.astype(BF16)
+        on_y[h] = start([remote(sum_y.at[1 - y_hi], from_y, far)])[0]
+
+    def last(h):
         if h == 0:
-            total = first_z[:, lat].astype(F32)
-            for d in range(nlat - 1):
-                total = total + last_x[d].astype(F32)
+            on_y[h].wait_recv()
+            total = sum_y[y_hi].astype(F32) + from_y[...].astype(F32)
         else:
-            total = sum_x[h - 1, :, z].astype(F32)
-            for d in range(nz - 1):
-                total = total + sum_z[h - 1, d].astype(F32)
-        sum_y[h] = total.astype(BF16)
-        on_y[h] = start([remote(sum_y.at[h, 1 - y_hi], from_y.at[h], far)])[0]
-
-    def last(h):
-        on_y[h].wait_recv()
-        total = sum_y[h, y_hi].astype(F32) + from_y[h].astype(F32)
+            for copy in on_second[h]:
+                copy.wait_recv()
+            total = sum_x[h - 1, lon].astype(F32)
+            for d in range(nlon - 1):
+                total = total + from_lon[h - 1, d].astype(F32)
         gqkv_ref[:, 192 * h : 192 * h + 192] = total[:, 0:192]
         gout_ref[:, 64 * h : 64 * h + 64] = total[:, 192:256]
 
@@ -306,7 +327,10 @@
         rows = pl.ds(at, size)
         to_side[rows] = (term[core, 1 - kind, rows].astype(F32) + from_core[1 - kind, rows].astype(F32)).astype(BF16)
         on_side += start([remote(to_side.at[rows], from_side.at[rows], side)])
+    onward(1)
     weight(3)
+    leave(3)
+    onward(2)
     tok_l[...] = dot(level_ref[core], tokc[...])
     cot_l[...] = dot(level_ref[core], cotc[...])
 
@@ -353,22 +377,21 @@
     first, middle, end = (pl.ds(*chunk) for chunk in chunks)
     finish(0)
     straight = start([remote(result.at[first], final.at[kind, core, first], {"lat": lat_up})])[0]
-    second(1)
     finish(1)
     spread_out[...] = dot(spread_ref[...], result[middle]).astype(BF16)
     returned = start([
         remote(spread_out.at[pl.ds(at, size)], back.at[pl.ds(at, size)], target)
         for at, size, target in ((0, 16, {"lat": lat_up}), (16, 32, {"lon": lon_up}), (48, 32, {"lat": lat_up, "lon": lon_up}))
     ])
-    leave(3)
+    second(1)
     finish(2)
+    onward(3)
     final[kind, core, end] = result[end]
     shared = {2: share(2)}
     straight.wait_recv()
     shared[0] = share(0)
     second(0)
     second(2)
-    third(1)
     for copy in returned:
         copy.wait_recv()
     back[U_ROWS : U_ROWS + CHUNK] = result[middle]
@@ -376,7 +399,6 @@
     shared[1] = share(1)
     place(kind, core)
     relayed = [relay(2, shared[2][0]), relay(0, shared[0][0])]
-    third(2)
     third(0)
     second(3)
     relayed.append(relay(1, shared[1][0]))
@@ -385,7 +407,6 @@
     for chunk in range(3):
         shared[chunk][1].wait_recv()
     place(kind, 1 - core)
-    third(3)
     for copy in relayed:
         copy.wait_recv()
     place(1 - kind, 1 - core)
@@ -404,7 +425,7 @@
     half = CELLS // LEV
     vmem = pl.BlockSpec(memory_space=pltpu.VMEM)
     hbm = pl.BlockSpec(memory_space=pl.ANY)
-    copies = 4 + 4 + 4 * (nlat - 1 + nz - 1 + 1) + 3 + 3 + 4 + 9
+    copies = 4 + 4 + (nlat - 1 + nz - 1 + 1) + 3 * (6 + nlon - 1) + 3 + 3 + 4 + 9
     shape = lambda *dims: pltpu.VMEM(dims, BF16)
     own, compact, level, spread, gather, natural, select, eye, cross = [jnp.asarray(t) for t in tables()]
     operands = (
@@ -432,14 +453,15 @@
             shape(CELLS, 768),
             shape(CELLS, 256),
             shape(4, 2, nz, nlat, rows, 256),
-            shape(3, nlat - 1, 2, nz, rows, 256),
-            shape(3, 2, nz, rows, 256),
+            *[shape(3, 2, nz, rows, 128)] * 4,
+            *[shape(3, 2, nz, rows, 256)] * 2,
+            shape(3, nlon, rows, 256),
+            shape(3, nlon - 1, rows, 256),
             shape(max(nz - 1, 1), 2, nlat, rows, 256),
             shape(2, nlat, rows, 256),
-            shape(3, max(nz - 1, 1), 2, rows, 256),
             shape(nlat - 1, 2, rows, 256),
-            shape(4, 2, rows, 256),
-            shape(4, rows, 256),
+            shape(2, rows, 256),
+            shape(rows, 256),
             shape(LEV, 2, T_ROWS, width),
             shape(2, T_ROWS, width),
             shape(T_ROWS, width),

time: 62.7 us -> 60.7 us (0.968)
  Pallas kernels: 58.6 us -> 57.1 us
    pallas_call x1, Pallas kernels: 58.6 us -> 57.1 us  [body(): pl.pallas_call(functools.partial(kernel, nlon, nlat), out_shape=(shape(LE...]
where the time goes in v5:
time: 60.7 us; the launch traced here: 60.6 us
  Pallas kernels  57.1 us (94%)
  local copies, waits for them, and re-layouts  2.86 us (5%)
  between operations  0.64 us (1%)
    pallas_call x1, Pallas kernels, body(): pl.pallas_call(functools.partial(kernel, nlon, nlat), out_shape=(shape(LE...  57.1 us
    unnamed x4, local copies, waits for them, and re-layouts  2.86 us

profile of v5, /device:TPU:1, one launch (start us, length us, event | category | flops | bytes accessed | tf_op | source)
XLA Modules:
  0.0 60.6 jit_solution(11679550898858750126)
XLA Ops:
  0.6 57.1 %shard_map.174 = (bf16[2,144,1024]{2,1,0:T(8,128)(2,1)S(1)}, bf16[2,144,1024]{2,1,0:T(8,128)(2,1)S(1)}, f32[16,768]{1,0:T(8,128)S(1)}, f32[16,256]{1,0:T(8,128)S(1)}) custom-call(bf16[288,1024]{1,0:T(8,128)(2,1)} %bitcast.10, bf16[288,1024]{1,0:T(8,128)(2,1)} %bitcast.11, bf16[320,288]{1,0:T(8,128)(2,1)} %constant.18.clone.own_in, f32[4,759]{1,0:T(4,128)} %bitcast.12, ...), custom_call_target="tpu_custom_call" | custom-call | tf_op jit(solution)/shard_map/pallas_call | solution.py:435
  57.7 0.8 %copy.23 = bf16[2,6,24,1024]{3,2,1,0:T(8,128)(2,1)} copy(bf16[2,6,24,1024]{3,2,1,0:T(8,128)(2,1)S(1)} %bitcast.8) | data formatting | bytes 1179648
  58.6 0.8 %copy.24 = bf16[2,6,24,1024]{3,2,1,0:T(8,128)(2,1)} copy(bf16[2,6,24,1024]{3,2,1,0:T(8,128)(2,1)S(1)} %bitcast.7) | data formatting | bytes 1179648
  59.4 0.6 copy.26
  60.0 0.6 %copy.25 = f32[16,768]{1,0:T(8,128)} copy(f32[16,768]{1,0:T(8,128)S(1)} %get-tuple-element.14) | data formatting | bytes 98304

commit v6 on v5

--- a/solution.py
+++ b/solution.py
@@ -91,7 +91,7 @@
     level_in, spread_in, gather_in, natural_in,
     layer_ref, dtok_ref, gqkv_ref, gout_ref,
     sent, held, tokc, cotc, normed, normed_t, cot_t, qkv, datt, wide_table, rolled, bias, dqkv, att,
-    wgt, relay_up, relay_down, added_up, added_down, from_below, from_above, sum_x, from_lon,
+    wgt, relay_up, relay_down, added_up, added_down, from_below, from_above, sum_x, rows_far, sum_far, from_far, sum_z, from_z,
     near_z, first_z, last_x, sum_y, from_y,
     term, from_core, to_side, from_side, tok_l, cot_l, result, spread_out, back, final,
     tok_ref, cot_ref, own_ref, table_ref, select_ref, cross_ref, compact_ref, gain_ref, wqkv_ref, wout_ref, eye_ref,
@@ -112,11 +112,10 @@
     z_down = [{"lon": y_hi * nz + (z + nz - d) % nz} for d in range(1, nz)]
     far = {"lon": (1 - y_hi) * nz + z}
 
-    lon_others = [{"lon": (lon + d) % nlon} for d in range(1, nlon)]
     opposite = (lat + 2) % nlat
 
-    sources = x_down + lon_others + [
-        sibling, side,
+    sources = x_down + z_down + [
+        far, sibling, side, {"lon": lon_up}, {"lon": lon_down},
         {"lat": lat_up, "lon": lon_up}, {"lat": lat_down, "lon": lon_down},
     ]
     barrier = pltpu.get_barrier_semaphore()
@@ -226,7 +225,8 @@
         dqkv[rows, first + 128 : first + 192] = dot(half, grad, 1, 0).astype(BF16)
 
     rows_out = wgt.shape[4]
-    on_relay, on_first, on_second, on_y = {}, {}, {}, {}
+    far_first = (1,)
+    on_relay, on_first, on_second, on_last, on_y = {}, {}, {}, {}, {}
     low, high = pl.ds(0, 128), pl.ds(128, 128)
 
     def weight(h):
@@ -275,14 +275,31 @@
             ])
         else:
             total = wgt[h, :, :, lat].astype(F32) + from_below[h - 1].astype(F32) + from_above[h - 1].astype(F32)
-            sum_x[h - 1] = total.astype(BF16).reshape(sum_x.shape[1:])
-            on_second[h] = start([
-                remote(sum_x.at[h - 1, target["lon"]], from_lon.at[h - 1, d], target) for d, target in enumerate(lon_others)
-            ])
+            sum_x[h - 1] = total.astype(BF16)
+            if h in far_first:
+                on_second[h] = start([remote(sum_x.at[h - 1, 1 - y_hi], rows_far.at[h - 1], far)])
+            else:
+                on_second[h] = start([
+                    remote(sum_x.at[h - 1, :, target["lon"] - y_hi * nz], from_z.at[h - 1, d], target) for d, target in enumerate(z_up)
+                ])
 
     def third(h):
         for copy in on_second[h]:
             copy.wait_recv()
+        if h in far_first:
+            total = sum_x[h - 1, y_hi].astype(F32) + rows_far[h - 1].astype(F32)
+            sum_far[h - 1] = total.astype(BF16)
+            on_last[h] = start([
+                remote(sum_far.at[h - 1, target["lon"] - y_hi * nz], from_z.at[h - 1, d, 0], target) for d, target in enumerate(z_up)
+            ])
+            return
+        if h > 0:
+            total = sum_x[h - 1, :, z].astype(F32)
+            for d in range(nz - 1):
+                total = total + from_z[h - 1, d].astype(F32)
+            sum_z[h - 1] = total.astype(BF16)
+            on_last[h] = start([remote(sum_z.at[h - 1, 1 - y_hi], from_far.at[h - 1], far)])
+            return
         total = first_z[:, lat].astype(F32)
         for d in range(nlat - 1):
             total = total + last_x[d].astype(F32)
@@ -294,15 +311,18 @@
             on_y[h].wait_recv()
             total = sum_y[y_hi].astype(F32) + from_y[...].astype(F32)
         else:
-            for copy in on_second[h]:
+            for copy in on_last[h]:
                 copy.wait_recv()
-            total = sum_x[h - 1, lon].astype(F32)
-            for d in range(nlon - 1):
-                total = total + from_lon[h - 1, d].astype(F32)
+            if h in far_first:
+                total = sum_far[h - 1, z].astype(F32)
+                for d in range(nz - 1):
+                    total = total + from_z[h - 1, d, 0].astype(F32)
+            else:
+                total = sum_z[h - 1, y_hi].astype(F32) + from_far[h - 1].astype(F32)
         gqkv_ref[:, 192 * h : 192 * h + 192] = total[:, 0:192]
         gout_ref[:, 64 * h : 64 * h + 64] = total[:, 192:256]
 
-    for h in range(4):
+    for h in (1, 0, 2, 3):
         for w in range(2):
             attend(w, h)
         if h < 3:
@@ -320,16 +340,16 @@
     on_core = start([
         remote(term.at[1 - core, :, pl.ds(at, size)], from_core.at[:, pl.ds(at, size)], sibling) for at, size in chunks
     ])
+    weight(3)
+    leave(3)
     sum_heads(core)
+    onward(1)
     on_side = []
     for copy, (at, size) in zip(on_core, chunks):
         copy.wait_recv()
         rows = pl.ds(at, size)
         to_side[rows] = (term[core, 1 - kind, rows].astype(F32) + from_core[1 - kind, rows].astype(F32)).astype(BF16)
         on_side += start([remote(to_side.at[rows], from_side.at[rows], side)])
-    onward(1)
-    weight(3)
-    leave(3)
     onward(2)
     tok_l[...] = dot(level_ref[core], tokc[...])
     cot_l[...] = dot(level_ref[core], cotc[...])
@@ -390,8 +410,9 @@
     shared = {2: share(2)}
     straight.wait_recv()
     shared[0] = share(0)
+    third(1)
+    second(2)
     second(0)
-    second(2)
     for copy in returned:
         copy.wait_recv()
     back[U_ROWS : U_ROWS + CHUNK] = result[middle]
@@ -399,19 +420,21 @@
     shared[1] = share(1)
     place(kind, core)
     relayed = [relay(2, shared[2][0]), relay(0, shared[0][0])]
+    second(3)
+    third(2)
     third(0)
-    second(3)
     relayed.append(relay(1, shared[1][0]))
+    third(3)
     place(1 - kind, core)
     last(1)
     for chunk in range(3):
         shared[chunk][1].wait_recv()
     place(kind, 1 - core)
+    last(2)
     for copy in relayed:
         copy.wait_recv()
     place(1 - kind, 1 - core)
     last(0)
-    last(2)
     last(3)
     for copy in started:
         copy.wait_send()
@@ -425,7 +448,7 @@
     half = CELLS // LEV
     vmem = pl.BlockSpec(memory_space=pltpu.VMEM)
     hbm = pl.BlockSpec(memory_space=pl.ANY)
-    copies = 4 + 4 + (nlat - 1 + nz - 1 + 1) + 3 * (6 + nlon - 1) + 3 + 3 + 4 + 9
+    copies = 4 + 4 + (nlat - 1 + nz - 1 + 1) + 3 * (6 + nz) + 3 + 3 + 4 + 9
     shape = lambda *dims: pltpu.VMEM(dims, BF16)
     own, compact, level, spread, gather, natural, select, eye, cross = [jnp.asarray(t) for t in tables()]
     operands = (
@@ -455,8 +478,12 @@
             shape(4, 2, nz, nlat, rows, 256),
             *[shape(3, 2, nz, rows, 128)] * 4,
             *[shape(3, 2, nz, rows, 256)] * 2,
-            shape(3, nlon, rows, 256),
-            shape(3, nlon - 1, rows, 256),
+            shape(3, 2, nz, rows, 256),
+            shape(3, nz, rows, 256),
+            shape(3, nz, rows, 256),
+            shape(3, rows, 256),
+            shape(3, 2, rows, 256),
+            shape(3, max(nz - 1, 1), 2, rows, 256),
             shape(max(nz - 1, 1), 2, nlat, rows, 256),
             shape(2, nlat, rows, 256),
             shape(nlat - 1, 2, rows, 256),

time: 60.7 us -> 59.2 us (0.975); the launches traced: 60.6 us -> 58.4 us
  Pallas kernels: 57.1 us -> 54.9 us
    pallas_call x1, Pallas kernels: 57.1 us -> 54.9 us  [body(): pl.pallas_call(functools.partial(kernel, nlon, nlat), out_shape=(shape(LE...]
where the time goes in v6:
time: 59.2 us; the launch traced here: 58.4 us
  Pallas kernels  54.9 us (93%)
  local copies, waits for them, and re-layouts  2.86 us (5%)
  between operations  0.64 us (1%)
    pallas_call x1, Pallas kernels, body(): pl.pallas_call(functools.partial(kernel, nlon, nlat), out_shape=(shape(LE...  54.9 us
    unnamed x4, local copies, waits for them, and re-layouts  2.86 us

profile of v6, /device:TPU:1, one launch (start us, length us, event | category | flops | bytes accessed | tf_op | source)
XLA Modules:
  0.0 58.4 jit_solution(14988965745206097709)
XLA Ops:
  0.6 54.9 %shard_map.174 = (bf16[2,144,1024]{2,1,0:T(8,128)(2,1)S(1)}, bf16[2,144,1024]{2,1,0:T(8,128)(2,1)S(1)}, f32[16,768]{1,0:T(8,128)S(1)}, f32[16,256]{1,0:T(8,128)S(1)}) custom-call(bf16[288,1024]{1,0:T(8,128)(2,1)} %bitcast.10, bf16[288,1024]{1,0:T(8,128)(2,1)} %bitcast.11, bf16[320,288]{1,0:T(8,128)(2,1)} %constant.18.clone.own_in, f32[4,759]{1,0:T(4,128)} %bitcast.12, ...), custom_call_target="tpu_custom_call" | custom-call | tf_op jit(solution)/shard_map/pallas_call | solution.py:458
  55.6 0.8 %copy.23 = bf16[2,6,24,1024]{3,2,1,0:T(8,128)(2,1)} copy(bf16[2,6,24,1024]{3,2,1,0:T(8,128)(2,1)S(1)} %bitcast.8) | data formatting | bytes 1179648
  56.4 0.8 %copy.24 = bf16[2,6,24,1024]{3,2,1,0:T(8,128)(2,1)} copy(bf16[2,6,24,1024]{3,2,1,0:T(8,128)(2,1)S(1)} %bitcast.7) | data formatting | bytes 1179648
  57.2 0.6 %copy.26 = f32[256,16]{0,1:T(8,128)} copy(f32[256,16]{0,1:T(8,128)S(1)} %bitcast.9) | data formatting | bytes 32768
  57.8 0.6 %copy.25 = f32[16,768]{1,0:T(8,128)} copy(f32[16,768]{1,0:T(8,128)S(1)} %get-tuple-element.14) | data formatting | bytes 98304

commit v7 on v6

--- a/solution.py
+++ b/solution.py
@@ -418,9 +418,9 @@
     back[U_ROWS : U_ROWS + CHUNK] = result[middle]
     final[kind, core, middle] = dot(gather_ref[...], back[...]).astype(BF16)
     shared[1] = share(1)
-    place(kind, core)
     relayed = [relay(2, shared[2][0]), relay(0, shared[0][0])]
     second(3)
+    place(kind, core)
     third(2)
     third(0)
     relayed.append(relay(1, shared[1][0]))

time: 59.2 us -> 59.2 us (level)
  no operation moved by 1% of the time
where the time goes in v7:
time: 59.2 us; the launch traced here: 58.4 us
  Pallas kernels  54.9 us (93%)
  local copies, waits for them, and re-layouts  2.86 us (5%)
  between operations  0.64 us (1%)
    pallas_call x1, Pallas kernels, body(): pl.pallas_call(functools.partial(kernel, nlon, nlat), out_shape=(shape(LE...  54.9 us
    unnamed x4, local copies, waits for them, and re-layouts  2.86 us

profile of v7, /device:TPU:1, one launch (start us, length us, event | category | flops | bytes accessed | tf_op | source)
XLA Modules:
  0.0 58.4 jit_solution(13226706442298193671)
XLA Ops:
  0.6 54.9 %shard_map.174 = (bf16[2,144,1024]{2,1,0:T(8,128)(2,1)S(1)}, bf16[2,144,1024]{2,1,0:T(8,128)(2,1)S(1)}, f32[16,768]{1,0:T(8,128)S(1)}, f32[16,256]{1,0:T(8,128)S(1)}) custom-call(bf16[288,1024]{1,0:T(8,128)(2,1)} %bitcast.10, bf16[288,1024]{1,0:T(8,128)(2,1)} %bitcast.11, bf16[320,288]{1,0:T(8,128)(2,1)} %constant.18.clone.own_in, f32[4,759]{1,0:T(4,128)} %bitcast.12, ...), custom_call_target="tpu_custom_call" | custom-call | tf_op jit(solution)/shard_map/pallas_call | solution.py:458
  55.6 0.8 %copy.23 = bf16[2,6,24,1024]{3,2,1,0:T(8,128)(2,1)} copy(bf16[2,6,24,1024]{3,2,1,0:T(8,128)(2,1)S(1)} %bitcast.8) | data formatting | bytes 1179648
  56.4 0.8 %copy.24 = bf16[2,6,24,1024]{3,2,1,0:T(8,128)(2,1)} copy(bf16[2,6,24,1024]{3,2,1,0:T(8,128)(2,1)S(1)} %bitcast.7) | data formatting | bytes 1179648
  57.2 0.6 %copy.26 = f32[256,16]{0,1:T(8,128)} copy(f32[256,16]{0,1:T(8,128)S(1)} %bitcast.9) | data formatting | bytes 32768
  57.8 0.6 %copy.25 = f32[16,768]{1,0:T(8,128)} copy(f32[16,768]{1,0:T(8,128)S(1)} %get-tuple-element.14) | data formatting | bytes 98304
